TPU v7x, 256 devices: a whole 4x4x8 slice. The times are simulated.
256 devices in a mesh: sp: 16 (over z, y_lo), tp: 16 (over y_hi, x, core).
Axes of the slice: x: 4, y: 4 (y_hi: 2, y_lo: 2; y = y_hi * 2 + y_lo), z: 8, core: 2. Of those that a mesh axis runs over, the one named last changes fastest.
Arguments:
- residual: bfloat16 [2048, 8192], P('sp', 'tp'), may hold values from -6 to 6
- queries: bfloat16 [2048, 8192], P(('tp', 'sp')), may hold values from -150 to 150
- keys: bfloat16 [2048, 1024], P(('tp', 'sp')), may hold values from -6 to 6
- values: bfloat16 [2048, 1024], P(('tp', 'sp')), may hold values from -24 to 24
- cache_keys: bfloat16 [16384, 1024], P('tp'), may hold values from -6 to 6
- cache_values: bfloat16 [16384, 1024], P('tp'), may hold values from -24 to 24
- offset: int32 [1], replicated, may hold values from 6144 to 16384
- w_out: bfloat16 [8192, 8192], P('sp', 'tp'), may hold values from -0.0625 to 0.0625
- norm_gain: bfloat16 [8192], P('tp'), may hold values from 0.099609375 to 1.8984375
- w_gate: bfloat16 [8192, 16384], P('tp', 'sp'), may hold values from -0.0625 to 0.0625
- w_up: bfloat16 [8192, 16384], P('tp', 'sp'), may hold values from -0.0625 to 0.0625
- w_down: bfloat16 [16384, 8192], P('sp', 'tp'), may hold values from -0.046875 to 0.046875
Outputs:
- block_out: bfloat16 [2048, 8192], P('sp', 'tp')
All inputs are finite; a program needn't handle non-finite values.
Results may differ from a plain program's by a relative error of at most 0.02.
Values may be sent and summed in bfloat16 or wider, within the bound.
A program may use at most 128 MiB of HBM per device.

v0:
```python
import math

import jax
import jax.numpy as jnp
from jax import lax
from jax.sharding import PartitionSpec as P

D = 8192
H = 64
KV = 8
HD = 128


def per_device(
    residual,
    queries,
    keys,
    values,
    cache_keys,
    cache_values,
    offset,
    w_out,
    norm_gain,
    w_gate,
    w_up,
    w_down,
):
    sp_count = lax.axis_size("sp")
    local_heads = H // sp_count
    shared_heads = max(KV // sp_count, 1)
    group = local_heads // shared_heads
    copies = max(sp_count // KV, 1)
    rows_in = queries.shape[0]
    keys_wide = jnp.repeat(keys.reshape(rows_in, KV, HD), copies, axis=1).reshape(
        rows_in, KV * copies * HD
    )
    values_wide = jnp.repeat(values.reshape(rows_in, KV, HD), copies, axis=1).reshape(
        rows_in, KV * copies * HD
    )
    query_heads, key_heads, value_heads = (
        lax.all_to_all(queries, "sp", split_axis=1, concat_axis=0, tiled=True),
        lax.all_to_all(keys_wide, "sp", split_axis=1, concat_axis=0, tiled=True),
        lax.all_to_all(values_wide, "sp", split_axis=1, concat_axis=0, tiled=True),
    )
    rows = query_heads.shape[0]
    sp_place = lax.axis_index("sp")
    tp_place = lax.axis_index("tp")
    first_shared = sp_place // (sp_count // KV)
    cache_k = lax.dynamic_slice_in_dim(cache_keys, first_shared * HD, shared_heads * HD, 1)
    cache_v = lax.dynamic_slice_in_dim(cache_values, first_shared * HD, shared_heads * HD, 1)
    cache_len = cache_keys.shape[0]
    joined = jnp.concatenate(
        [jnp.concatenate([cache_k, cache_v], 1), jnp.concatenate([key_heads, value_heads], 1)], 0
    )
    period = cache_len + rows
    query_blocks = query_heads.reshape(rows, shared_heads, group, HD)
    query_index = tp_place * rows + jnp.arange(rows, dtype=jnp.int32)
    context_end = offset[0]
    score_scale = 1.0 / HD**0.5

    def fold_block(carry, block, start):
        running_max, running_sum, summed = carry
        block_len = block.shape[0]
        positions = start + jnp.arange(block_len, dtype=jnp.int32)
        owner_shard = positions // period
        within = positions % period
        from_cache = within < cache_len
        cache_pos = owner_shard * cache_len + within
        new_pos = owner_shard * rows + within - cache_len
        visible = jnp.where(
            from_cache[None, :],
            (cache_pos < context_end)[None, :],
            new_pos[None, :] <= query_index[:, None],
        )
        key_piece = block[:, : shared_heads * HD].reshape(block_len, shared_heads, HD)
        value_piece = block[:, shared_heads * HD :].reshape(block_len, shared_heads, HD)
        scores = jnp.einsum(
            "rkgd,nkd->kgrn", query_blocks, key_piece, preferred_element_type=jnp.float32
        )
        scores = scores.reshape(local_heads, rows, block_len) * score_scale
        piece_max = jnp.max(jnp.where(visible[None], scores, -1e30), axis=2)
        new_max = jnp.maximum(running_max, piece_max)
        weights = jnp.where(visible[None], jnp.exp(scores - new_max[:, :, None]), 0.0)
        factor = jnp.exp(running_max - new_max)
        new_sum = running_sum * factor + jnp.sum(weights, axis=2)
        update = jnp.einsum(
            "kgrn,nkd->kgrd",
            weights.astype(jnp.bfloat16).reshape(shared_heads, group, rows, block_len),
            value_piece,
            preferred_element_type=jnp.float32,
        )
        new_summed = summed * factor[:, :, None] + update.reshape(local_heads, rows, HD)
        return (new_max, new_sum, new_summed)

    initial = (
        jnp.full((local_heads, rows), -1e30, jnp.float32),
        jnp.zeros((local_heads, rows), jnp.float32),
        jnp.zeros((local_heads, rows, HD), jnp.float32),
    )
    piece = lax.all_gather(joined, "tp", axis=0, tiled=True)
    piece_len = piece.shape[0]
    step_len = math.gcd(piece_len, 1024)
    turns = piece_len // step_len

    def one_step(index, inner):
        first = (index * step_len).astype(jnp.int32)
        block = lax.dynamic_slice_in_dim(piece, first, step_len, 0)
        return fold_block(inner, block, first)

    final_max, final_sum, final_summed = lax.fori_loop(0, turns, one_step, initial)
    attended = (final_summed / final_sum[:, :, None]).astype(jnp.bfloat16)
    attended = jnp.transpose(attended, (1, 0, 2)).reshape(rows, local_heads * HD)
    attended_all = lax.all_gather(attended, "tp", axis=0, tiled=True)
    attn_out = lax.psum_scatter(
        jnp.dot(attended_all, w_out, preferred_element_type=jnp.float32).astype(jnp.bfloat16),
        "sp",
        scatter_dimension=0,
        tiled=True,
    ).astype(jnp.float32)
    stream = (residual.astype(jnp.float32) + attn_out).astype(jnp.bfloat16)
    wide = stream.astype(jnp.float32)
    squares = lax.psum(jnp.sum(wide * wide, axis=1), "tp")
    scale_rows = lax.rsqrt(squares / D + 1e-06)
    normed = (wide * scale_rows[:, None] * norm_gain.astype(jnp.float32)[None, :]).astype(
        jnp.bfloat16
    )
    normed_all = lax.all_gather(normed, "sp", axis=0, tiled=True)
    both_weights = jnp.concatenate([w_gate, w_up], 1)
    width = w_gate.shape[1]
    both = lax.psum_scatter(
        jnp.dot(normed_all, both_weights, preferred_element_type=jnp.float32).astype(jnp.bfloat16),
        "tp",
        scatter_dimension=0,
        tiled=True,
    ).astype(jnp.float32)
    hidden = (jax.nn.silu(both[:, :width]) * both[:, width:]).astype(jnp.bfloat16)
    hidden_all = lax.all_gather(hidden, "tp", axis=0, tiled=True)
    down = lax.psum_scatter(
        jnp.dot(hidden_all, w_down, preferred_element_type=jnp.float32).astype(jnp.bfloat16),
        "sp",
        scatter_dimension=0,
        tiled=True,
    ).astype(jnp.float32)
    return (wide + down).astype(jnp.bfloat16)


def solution(mesh):
    in_specs = (
        P("sp", "tp"),
        P(("tp", "sp"), None),
        P(("tp", "sp"), None),
        P(("tp", "sp"), None),
        P("tp", None),
        P("tp", None),
        P(),
        P("sp", "tp"),
        P("tp"),
        P("tp", "sp"),
        P("tp", "sp"),
        P("sp", "tp"),
    )
    out_specs = P("sp", "tp")
    return jax.shard_map(
        per_device, mesh=mesh, in_specs=in_specs, out_specs=out_specs, check_vma=False
    )
```

profile of v0, /device:TPU:1, one launch (start us, length us, event | category | flops | bytes accessed | tf_op | source)
XLA Modules:
  0.0 721.5 jit_solution(12759123512578131365)
XLA Ops:
  8.0 10.1 %all-to-all-start = ((bf16[8,16,128]{2,0,1:T(8,128)(2,1)}), bf16[8,16,128]{2,0,1:T(8,128)(2,1)S(1)}, u32[]{:S(2)}, u32[]{:S(2)}) async-start(bf16[8,16,128]{2,0,1:T(8,128)(2,1)} %bitcast.2), calls=%async_computation | async-start | bytes 65536 | tf_op jit(solution)/shard_map/all_to_all | solution.py:42
  18.1 7.6 %all-to-all-done = bf16[8,16,128]{2,0,1:T(8,128)(2,1)S(1)} async-done(((bf16[8,16,128]{2,0,1:T(8,128)(2,1)}), bf16[8,16,128]{2,0,1:T(8,128)(2,1)S(1)}, u32[]{:S(2)}, u32[]{:S(2)}) %all-to-all-start) | async-done | bytes 32800 | tf_op jit(solution)/shard_map/all_to_all | solution.py:42
  27.1 3.5 all-to-all-start.1
  31.7 6.4 all-to-all-done.1
  39.1 3.5 all-to-all-start.2
  42.7 8.4 %all-to-all-done.2 = bf16[8,16,512]{2,0,1:T(8,128)(2,1)S(1)} async-done(((bf16[8,16,512]{2,0,1:T(8,128)(2,1)}), bf16[8,16,512]{2,0,1:T(8,128)(2,1)S(1)}, u32[]{:S(2)}, u32[]{:S(2)}) %all-to-all-start.2) | async-done | bytes 131104 | tf_op jit(solution)/shard_map/all_to_all | solution.py:41
  51.2 69.3 %all-gather.5.cloned.1.call-done = bf16[18432,256]{1,0:T(8,128)(2,1)} async-done(((bf16[1152,256]{1,0:T(8,128)(2,1)}), bf16[18432,256]{1,0:T(8,128)(2,1)}) %all-gather.5.cloned.1.call-update) | async-done | bytes 9437200 | tf_op jit(solution)/shard_map/all_gather | solution.py:100
  120.5 106.6 %while.20 = (s32[]{:T(128)}, f32[4,128]{1,0:T(4,128)S(1)}, f32[4,128]{1,0:T(4,128)S(1)}, f32[4,128,128]{2,1,0:T(8,128)}, s32[]{:T(128)}, /*index=5*/bf16[18432,2...) while((s32[]{:T(128)}, f32[4,128]{1,0:T(4,128)S(1)}, ...), condition=%wide.region_3.4_spmd.clone, body=%wide.region_0.3_spmd.clone.sunk | while | flops 274697856 | bytes 8041695 | solution.py:110
  129.9 2.4 convolution_add_fusion.2
  147.6 2.4 convolution_add_fusion.2
  165.4 2.4 convolution_add_fusion.2
  183.2 2.4 convolution_add_fusion.2
  201.0 2.4 convolution_add_fusion.2
  218.8 2.4 convolution_add_fusion.2
  229.0 52.7 %all-gather.7.cloned.1.call-done = bf16[2048,512]{0,1:T(8,128)(2,1)} async-done(((bf16[128,512]{0,1:T(8,128)(2,1)}), bf16[2048,512]{0,1:T(8,128)(2,1)}) %all-gather.7.cloned.1.call-update) | async-done | bytes 2097168 | tf_op jit(solution)/shard_map/all_gather | solution.py:113
  281.7 4.3 convolution_convert_fusion.2
  286.6 61.2 %reduce-scatter.4.cloned.1.call-done = bf16[128,512]{1,0:T(8,128)(2,1)} async-done(((bf16[2048,512]{1,0:T(8,128)(2,1)}), bf16[128,512]{1,0:T(8,128)(2,1)}) %reduce-scatter.4.cloned.1.call-update) | async-done | bytes 131088 | tf_op jit(solution)/shard_map/reduce_scatter | solution.py:114
  348.9 44.6 %psum.7 = f32[128]{0:T(128)S(1)} all-reduce(f32[128]{0:T(128)S(1)} %fusion.31), channel_id=1, replica_groups=mesh['sp'=16,'tp'=16] {'tp'}, use_global_device_ids=true, to_apply=%region_6.7 | all-reduce | flops 128 | bytes 1024 | tf_op jit(solution)/shard_map/psum | solution.py:122
  395.2 60.8 %all-gather.9.cloned.1.call-done = bf16[2048,512]{1,0:T(8,128)(2,1)} async-done(((bf16[128,512]{1,0:T(8,128)(2,1)}), bf16[2048,512]{1,0:T(8,128)(2,1)}) %all-gather.9.cloned.1.call-update) | async-done | bytes 2097168 | tf_op jit(solution)/shard_map/all_gather | solution.py:127
  456.0 8.5 %convolution_convert_fusion = bf16[2048,2048]{1,0:T(8,128)(2,1)} fusion(bf16[2048,512]{1,0:T(8,128)(2,1)} %all-gather.9.cloned.1.call-done, bf16[512,1024]{1,0:T(8,128)(2,1)S(1)} %copy-done.4, bf16[512,1024]{1,0:T(8,128)(2,1)S(1)} %copy-done.5), kind=kOutput, calls=%fused_computation.43 | convolution fusion | flops 4303355904 | bytes 12582912 | tf_op jit(solution)/shard_map/dot_general | solution.py:131
  464.6 116.3 %reduce-scatter.6.cloned.1.call-done = bf16[128,2048]{1,0:T(8,128)(2,1)} async-done(((bf16[2048,2048]{1,0:T(8,128)(2,1)}), bf16[128,2048]{1,0:T(8,128)(2,1)}) %reduce-scatter.6.cloned.1.call-update) | async-done | bytes 524304 | tf_op jit(solution)/shard_map/reduce_scatter | solution.py:130
  583.0 62.1 %all-gather.11.cloned.1.call-done = bf16[2048,1024]{1,0:T(8,128)(2,1)} async-done(((bf16[128,1024]{1,0:T(8,128)(2,1)}), bf16[2048,1024]{1,0:T(8,128)(2,1)}) %all-gather.11.cloned.1.call-update) | async-done | bytes 4194320 | tf_op jit(solution)/shard_map/all_gather | solution.py:137
  645.2 5.9 convolution_convert_fusion.1
  651.1 61.9 %reduce-scatter.8.cloned.1.call-done = bf16[128,512]{1,0:T(8,128)(2,1)} async-done(((bf16[2048,512]{1,0:T(8,128)(2,1)}), bf16[128,512]{1,0:T(8,128)(2,1)}) %reduce-scatter.8.cloned.1.call-update) | async-done | bytes 131088 | tf_op jit(solution)/shard_map/reduce_scatter | solution.py:138
  (218 shorter events, 105.0 us)
Async XLA Ops:
  6.5 638.6 %copy-start = (bf16[1024,512]{1,0:T(8,128)(2,1)S(1)}, bf16[1024,512]{1,0:T(8,128)(2,1)}, u32[]{:S(2)}) copy-start(bf16[1024,512]{1,0:T(8,128)(2,1)} %param.25) | copy-start | bytes 3145732
  8.0 17.8 %all-to-all-start = ((bf16[8,16,128]{2,0,1:T(8,128)(2,1)}), bf16[8,16,128]{2,0,1:T(8,128)(2,1)S(1)}, u32[]{:S(2)}, u32[]{:S(2)}) async-start(bf16[8,16,128]{2,0,1:T(8,128)(2,1)} %bitcast.2), calls=%async_computation | async-start | bytes 65536 | tf_op jit(solution)/shard_map/all_to_all | solution.py:42
  27.1 11.1 %all-to-all-start.1 = ((bf16[8,16,128]{2,0,1:T(8,128)(2,1)}), bf16[8,16,128]{2,0,1:T(8,128)(2,1)S(1)}, u32[]{:S(2)}, u32[]{:S(2)}) async-start(bf16[8,16,128]{2,0,1:T(8,128)(2,1)} %bitcast.6), calls=%async_computation.1 | async-start | bytes 65536 | tf_op jit(solution)/shard_map/all_to_all | solution.py:43
  30.6 89.9 %all-gather.5.cloned.1.call-start = ((), (), s32[]{:S(2)}) async-start(), calls=%async_computation.6 | async-start | bytes 10027008 | tf_op jit(solution)/shard_map/all_gather | solution.py:100
  39.1 12.0 %all-to-all-start.2 = ((bf16[8,16,512]{2,0,1:T(8,128)(2,1)}), bf16[8,16,512]{2,0,1:T(8,128)(2,1)S(1)}, u32[]{:S(2)}, u32[]{:S(2)}) async-start(bf16[8,16,512]{2,0,1:T(8,128)(2,1)} %bitcast.9), calls=%async_computation.2 | async-start | bytes 262144 | tf_op jit(solution)/shard_map/all_to_all | solution.py:41
  42.6 239.1 %all-gather.7.cloned.1.call-start = ((), (), s32[]{:S(2)}) async-start(), calls=%async_computation.7 | async-start | bytes 2228224 | tf_op jit(solution)/shard_map/all_gather | solution.py:113
  228.9 118.9 %reduce-scatter.4.cloned.1.call-start = ((), (), s32[]{:S(2)}) async-start(), calls=%async_computation.8 | async-start | bytes 2228224 | tf_op jit(solution)/shard_map/reduce_scatter | solution.py:114
  286.0 0.7 copy-start.3
  286.0 61.9 %copy-start.1 = (bf16[128,512]{1,0:T(8,128)(2,1)S(1)}, bf16[128,512]{1,0:T(8,128)(2,1)}, u32[]{:S(2)}) copy-start(bf16[128,512]{1,0:T(8,128)(2,1)} %param.14) | copy-start | bytes 393220
  286.0 170.0 %copy-start.4 = (bf16[512,1024]{1,0:T(8,128)(2,1)S(1)}, bf16[512,1024]{1,0:T(8,128)(2,1)}, u32[]{:S(2)}) copy-start(bf16[512,1024]{1,0:T(8,128)(2,1)} %param.24) | copy-start | bytes 3145732
  286.0 170.0 %copy-start.5 = (bf16[512,1024]{1,0:T(8,128)(2,1)S(1)}, bf16[512,1024]{1,0:T(8,128)(2,1)}, u32[]{:S(2)}) copy-start(bf16[512,1024]{1,0:T(8,128)(2,1)} %param.23) | copy-start | bytes 3145732
  286.0 170.0 %all-gather.9.cloned.1.call-start = ((), (), s32[]{:S(2)}) async-start(), calls=%async_computation.9 | async-start | bytes 2228224 | tf_op jit(solution)/shard_map/all_gather | solution.py:127
  395.2 185.8 %reduce-scatter.6.cloned.1.call-start = ((), (), s32[]{:S(2)}) async-start(), calls=%async_computation.10 | async-start | bytes 8912896 | tf_op jit(solution)/shard_map/reduce_scatter | solution.py:130
  464.6 180.6 %all-gather.11.cloned.1.call-start = ((), (), s32[]{:S(2)}) async-start(), calls=%async_computation.11 | async-start | bytes 4456448 | tf_op jit(solution)/shard_map/all_gather | solution.py:137
  583.0 130.0 %reduce-scatter.8.cloned.1.call-start = ((), (), s32[]{:S(2)}) async-start(), calls=%async_computation.12 | async-start | bytes 2228224 | tf_op jit(solution)/shard_map/reduce_scatter | solution.py:138
  651.0 62.0 %copy-start.2 = (bf16[128,512]{1,0:T(8,128)(2,1)S(1)}, bf16[128,512]{1,0:T(8,128)(2,1)}, u32[]{:S(2)}) copy-start(bf16[128,512]{1,0:T(8,128)(2,1)} %reduce-scatter.4.cloned.1.call-done) | copy-start | bytes 393220
Sparse Core Ops, SparseCore 0:
  39.2 81.2 all-gather.4
  229.1 52.5 all-gather.6
  286.1 61.6 reduce-scatter.3
  395.3 60.6 all-gather.8
  464.7 116.1 reduce-scatter.5
  583.5 61.5 all-gather.10
  651.2 61.7 reduce-scatter.7
where the time goes:
time: 734 us; the launch traced here: 721 us
  waiting for transfers between devices  507 us (69%)
  matrix products  87.7 us (12%)
  other arithmetic  44.6 us (6%)
  blocking collectives  44.6 us (6%)
  starting transfers between devices  17.4 us (2%)
  between operations  13.6 us (2%)
    reduce_scatter x1, waiting for transfers between devices, per_device(): lax.psum_scatter(jnp.dot(normed_all, both_weights, preferred_element_type...  116 us
    all_gather x1, waiting for transfers between devices, per_device(): piece = lax.all_gather(joined, 'tp', axis=0, tiled=True)  69.3 us
    all_gather x1, waiting for transfers between devices, per_device(): hidden_all = lax.all_gather(hidden, 'tp', axis=0, tiled=True)  62.1 us
    reduce_scatter x1, waiting for transfers between devices, per_device(): lax.psum_scatter(jnp.dot(hidden_all, w_down, preferred_element_type=jnp.f...  61.9 us
    reduce_scatter x1, waiting for transfers between devices, per_device(): lax.psum_scatter(jnp.dot(attended_all, w_out, preferred_element_type=jnp....  61.2 us
    all_gather x1, waiting for transfers between devices, per_device(): normed_all = lax.all_gather(normed, 'sp', axis=0, tiled=True)  60.8 us
    all_gather x1, waiting for transfers between devices, per_device(): attended_all = lax.all_gather(attended, 'tp', axis=0, tiled=True)  52.7 us
    psum x1, blocking collectives, per_device(): squares = lax.psum(jnp.sum(wide * wide, axis=1), 'tp')  44.6 us
  transfers between devices with their start and end apart: 10, of which 10 were waited for; matrix products, arithmetic and copies ran while one was open for 0% of the time, Pallas kernels for 0%

commit v1 on v0

v1 whole, which is shorter than its diff:
```python
import functools

import jax
import jax.numpy as jnp
from jax import lax
from jax.experimental import pallas as pl
from jax.experimental.pallas import tpu as pltpu
from jax.sharding import PartitionSpec as P

D = 8192
H = 64
KV = 8
HD = 128
EPS = 1e-6
BF = jnp.bfloat16
F32 = jnp.float32
MESH = pl.DeviceIdType.MESH
VM = pltpu.VMEM
DMA = pltpu.SemaphoreType.DMA
SCORE_SCALE = 1.4426950408889634 / HD**0.5
LOWEST = -1e30
VMEM_LIMIT = 56 * 2**20


def here():
    return lax.axis_index("sp"), lax.axis_index("tp")


def remote(src, dst, send, recv, device):
    return pltpu.make_async_remote_copy(
        src_ref=src,
        dst_ref=dst,
        send_sem=send,
        recv_sem=recv,
        device_id=device,
        device_id_type=MESH,
    )


def chip_at(tp, k, sign):
    chip = tp // 2
    high = (chip // 4 + k // 4) % 2
    x = (chip % 4 + 4 + sign * (k % 4)) % 4
    return (high * 4 + x) * 2 + tp % 2


def greet(devices):
    barrier = pltpu.get_barrier_semaphore()
    for device in devices:
        pl.semaphore_signal(barrier, inc=1, device_id=device, device_id_type=MESH)
    pl.semaphore_wait(barrier, len(devices))


def gather_tp(own_ref, all_ref, same_send, same_recv, pair_send, pair_recv):
    sp, tp = here()
    sibling = (sp, tp + 1 - 2 * (tp % 2))
    for k in range(1, 8):
        remote(own_ref, all_ref.at[tp], same_send.at[k], same_recv.at[k], (sp, chip_at(tp, k, 1))).start()
    remote(own_ref, all_ref.at[tp], pair_send.at[0], pair_recv.at[0], sibling).start()
    all_ref[tp] = own_ref[...]

    def forward(k, _):
        source = chip_at(tp, k, -1)
        block = all_ref.at[source]
        remote(block, block, same_send.at[k], same_recv.at[k], sibling).wait_recv()
        remote(block, block, pair_send.at[k], pair_recv.at[k], sibling).start()
        return 0

    lax.fori_loop(1, 8, forward, 0)

    def settle(k, _):
        source = chip_at(tp, k, -1)
        other = all_ref.at[source + 1 - 2 * (tp % 2)]
        remote(other, other, pair_send.at[k], pair_recv.at[k], sibling).wait_recv()
        remote(own_ref, other, pair_send.at[k], pair_recv.at[k], sibling).wait_send()
        return 0

    lax.fori_loop(0, 8, settle, 0)

    def sent(k, _):
        remote(own_ref, all_ref.at[tp], same_send.at[k], same_recv.at[k], sibling).wait_send()
        return 0

    lax.fori_loop(1, 8, sent, 0)


def attention_kernel(
    offset_ref,
    message_ref,
    cache_k_ref,
    cache_v_ref,
    w_gate_ref,
    w_up_ref,
    attended_ref,
    other_gate_ref,
    other_up_ref,
    received,
    keys,
    vals,
    new_keys,
    new_vals,
    vals_t,
    queries,
    own,
    out_send,
    out_recv,
    stat_send,
    stat_recv,
    a2a_send,
    a2a_recv,
    local_sem,
    pair_send,
    pair_recv,
    q_send,
    q_recv,
    o_send,
    o_recv,
    st_send,
    st_recv,
    ag_send,
    ag_recv,
    fw_send,
    fw_recv,
):
    sp, tp = here()
    core = tp % 2
    chip = tp // 2
    sibling = (sp, tp + 1 - 2 * core)
    greet(
        [((sp + j) % 16, tp) for j in range(1, 16)]
        + [(sp, chip_at(tp, k, 1)) for k in range(1, 8)]
        + [sibling]
    )

    def exchange(j, _):
        target = (sp + j) % 16
        remote(message_ref.at[target], received.at[sp], a2a_send.at[j], a2a_recv.at[j], (target, tp)).start()
        return 0

    lax.fori_loop(1, 16, exchange, 0)
    columns = pl.ds(pl.multiple_of((sp // 2) * HD, HD), HD)
    local_k = pltpu.make_async_copy(cache_k_ref.at[:, columns], keys.at[core], local_sem.at[0])
    local_v = pltpu.make_async_copy(cache_v_ref.at[:, columns], vals.at[core], local_sem.at[1])
    local_k.start()
    local_v.start()
    pair_k = remote(cache_k_ref.at[:, columns], keys.at[core], pair_send.at[0], pair_recv.at[0], sibling)
    pair_v = remote(cache_v_ref.at[:, columns], vals.at[core], pair_send.at[1], pair_recv.at[1], sibling)
    pair_k.start()
    pair_v.start()
    received[sp] = message_ref[sp]

    def arrived(j, _):
        source = (sp + 16 - j) % 16
        block = received.at[source]
        remote(block, block, a2a_send.at[j], a2a_recv.at[j], sibling).wait()
        return 0

    lax.fori_loop(1, 16, arrived, 0)
    queries[0] = received[:, :32, :].reshape(512, HD)

    def ask(k, _):
        remote(queries.at[0], queries.at[k], q_send.at[k], q_recv.at[k], (sp, chip_at(tp, k, 1))).start()
        return 0

    lax.fori_loop(1, 8, ask, 0)
    fresh = received[:, 32:, :].astype(F32).reshape(16, 2, 8, HD)
    new_keys[core] = fresh[:, 0].reshape(HD, HD).astype(BF)
    new_vals[core] = fresh[:, 1].reshape(HD, HD).astype(BF)
    pair_nk = remote(new_keys.at[core], new_keys.at[core], pair_send.at[2], pair_recv.at[2], sibling)
    pair_nv = remote(new_vals.at[core], new_vals.at[core], pair_send.at[3], pair_recv.at[3], sibling)
    pair_nk.start()
    pair_nv.start()
    local_k.wait()
    local_v.wait()
    for copy in (pair_k, pair_v, pair_nk, pair_nv):
        copy.wait()
    pair_g = remote(w_gate_ref, other_gate_ref, pair_send.at[4], pair_recv.at[4], sibling)
    pair_u = remote(w_up_ref, other_up_ref, pair_send.at[5], pair_recv.at[5], sibling)
    pair_g.start()
    pair_u.start()
    for half in range(2):
        for piece in range(4):
            rows = vals[half, piece * 256 : piece * 256 + 256, :].astype(F32)
            vals_t[:, half * 1024 + piece * 256 : half * 1024 + piece * 256 + 256] = rows.T.astype(BF)
    vals_t[:, 2048:2304] = new_vals[...].reshape(256, HD).astype(F32).T.astype(BF)
    cached = offset_ref[0] - chip * 2048
    step = 512

    def attend(k, _):
        asker = chip_at(tp, k, -1)

        @pl.when(k > 0)
        def _():
            remote(queries.at[k], queries.at[k], q_send.at[k], q_recv.at[k], sibling).wait()

        q = queries[k]
        top = jnp.full((1, 512), LOWEST, F32)
        total = jnp.zeros((1, 512), F32)
        summed = jnp.zeros((HD, 512), F32)
        for first in range(0, 2304, step):
            if first < 2048:
                block = keys[first // 1024, first % 1024 : first % 1024 + step, :]
            else:
                block = new_keys[...].reshape(256, HD)
            scores = lax.dot_general(block, q, (((1,), (1,)), ((), ())), preferred_element_type=F32)
            count = block.shape[0]
            place = lax.broadcasted_iota(jnp.int32, (count, 512), 0)
            if first < 2048:
                scores = jnp.where(place < cached - first, scores, LOWEST)
            else:
                lane = lax.broadcasted_iota(jnp.int32, (count, 512), 1)
                token = (lane // 32) * 8 + lane % 8
                scores = jnp.where(place - token <= asker * 128 - chip * 256, scores, LOWEST)
            higher = jnp.maximum(top, jnp.max(scores, axis=0, keepdims=True))
            weights = jnp.exp2((scores - higher) * SCORE_SCALE)
            factor = jnp.exp2((top - higher) * SCORE_SCALE)
            total = total * factor + jnp.sum(weights, axis=0, keepdims=True)
            summed = summed * factor + jnp.dot(
                vals_t[:, first : first + count], weights.astype(BF), preferred_element_type=F32
            )
            top = higher
        out_send[k] = summed.astype(BF)
        stat_send[k] = jnp.concatenate([jnp.broadcast_to(top, (4, 512)), jnp.broadcast_to(total, (4, 512))], 0)

        @pl.when(k > 0)
        def _():
            remote(out_send.at[k], out_recv.at[k], o_send.at[k], o_recv.at[k], (sp, asker)).start()
            remote(stat_send.at[k], stat_recv.at[k], st_send.at[k], st_recv.at[k], (sp, asker)).start()

        return 0

    lax.fori_loop(0, 8, attend, 0)

    def collect(k, _):
        remote(out_send.at[k], out_recv.at[k], o_send.at[k], o_recv.at[k], sibling).wait()
        remote(stat_send.at[k], stat_recv.at[k], st_send.at[k], st_recv.at[k], sibling).wait()
        return 0

    lax.fori_loop(1, 8, collect, 0)
    tops = [stat_send[0, 0:1, :]] + [stat_recv[k, 0:1, :] for k in range(1, 8)]
    highest = functools.reduce(jnp.maximum, tops)
    shares = [jnp.exp2((top - highest) * SCORE_SCALE) for top in tops]
    total = stat_send[0, 4:5, :] * shares[0]
    summed = out_send[0].astype(F32) * shares[0]
    for k in range(1, 8):
        total = total + stat_recv[k, 4:5, :] * shares[k]
        summed = summed + out_recv[k].astype(F32) * shares[k]
    mixed = (summed / total).T.reshape(16, 4, 8, HD)
    for h in range(4):
        own[:, h * HD : (h + 1) * HD] = mixed[:, h].reshape(HD, HD).astype(BF)
    gather_tp(own, attended_ref, ag_send, ag_recv, fw_send, fw_recv)
    pair_g.wait()
    pair_u.wait()


def params(number):
    return pltpu.CompilerParams(
        collective_id=number, has_side_effects=True, vmem_limit_bytes=VMEM_LIMIT
    )


def in_vmem(count):
    return [pl.BlockSpec(memory_space=pltpu.VMEM)] * count


def anywhere(count):
    return [pl.BlockSpec(memory_space=pl.ANY)] * count


def run_attention(offset, message, cache_keys, cache_values, w_gate, w_up):
    return pl.pallas_call(
        attention_kernel,
        out_shape=(
            jax.ShapeDtypeStruct((16, 128, 512), BF),
            jax.ShapeDtypeStruct(w_gate.shape, BF),
            jax.ShapeDtypeStruct(w_up.shape, BF),
        ),
        in_specs=[pl.BlockSpec(memory_space=pltpu.SMEM)] + in_vmem(1) + anywhere(4),
        out_specs=tuple(in_vmem(1) + anywhere(2)),
        scratch_shapes=[
            VM((16, 48, HD), BF),
            VM((2, 1024, HD), BF),
            VM((2, 1024, HD), BF),
            VM((2, 128, HD), BF),
            VM((2, 128, HD), BF),
            VM((HD, 2304), BF),
            VM((8, 512, HD), BF),
            VM((128, 512), BF),
            VM((8, HD, 512), BF),
            VM((8, HD, 512), BF),
            VM((8, 8, 512), F32),
            VM((8, 8, 512), F32),
            DMA((16,)),
            DMA((16,)),
            DMA((2,)),
            DMA((6,)),
            DMA((6,)),
        ]
        + [DMA((8,))] * 10,
        compiler_params=params(0),
        name="attention",
    )(offset, message, cache_keys, cache_values, w_gate, w_up)


def per_device(
    residual,
    queries,
    keys,
    values,
    cache_keys,
    cache_values,
    offset,
    w_out,
    norm_gain,
    w_gate,
    w_up,
    w_down,
):
    asked = jnp.transpose(queries.reshape(8, 16, 4, HD), (1, 2, 0, 3)).reshape(16, 32, HD)
    pairs = jnp.stack([keys.reshape(8, KV, HD), values.reshape(8, KV, HD)], 0)
    pairs = jnp.transpose(pairs, (2, 0, 1, 3)).reshape(KV, 16, HD)
    message = jnp.concatenate([asked, jnp.repeat(pairs, 2, axis=0)], 1)
    attended_all, other_gate, other_up = run_attention(
        offset, message, cache_keys, cache_values, w_gate, w_up
    )
    attended_all = attended_all.reshape(2048, 512)
    attn_out = lax.psum_scatter(
        jnp.dot(attended_all, w_out, preferred_element_type=jnp.float32).astype(jnp.bfloat16),
        "sp",
        scatter_dimension=0,
        tiled=True,
    ).astype(jnp.float32)
    stream = (residual.astype(jnp.float32) + attn_out).astype(jnp.bfloat16)
    wide = stream.astype(jnp.float32)
    squares = lax.psum(jnp.sum(wide * wide, axis=1), "tp")
    scale_rows = lax.rsqrt(squares / D + 1e-06)
    normed = (wide * scale_rows[:, None] * norm_gain.astype(jnp.float32)[None, :]).astype(
        jnp.bfloat16
    )
    normed_all = lax.all_gather(normed, "sp", axis=0, tiled=True)
    both_weights = jnp.concatenate([w_gate, w_up], 1)
    width = w_gate.shape[1]
    both = lax.psum_scatter(
        jnp.dot(normed_all, both_weights, preferred_element_type=jnp.float32).astype(jnp.bfloat16),
        "tp",
        scatter_dimension=0,
        tiled=True,
    ).astype(jnp.float32)
    hidden = (jax.nn.silu(both[:, :width]) * both[:, width:]).astype(jnp.bfloat16)
    hidden_all = lax.all_gather(hidden, "tp", axis=0, tiled=True)
    down = lax.psum_scatter(
        jnp.dot(hidden_all, w_down, preferred_element_type=jnp.float32).astype(jnp.bfloat16),
        "sp",
        scatter_dimension=0,
        tiled=True,
    ).astype(jnp.float32)
    return (wide + down).astype(jnp.bfloat16)


def solution(mesh):
    in_specs = (
        P("sp", "tp"),
        P(("tp", "sp"), None),
        P(("tp", "sp"), None),
        P(("tp", "sp"), None),
        P("tp", None),
        P("tp", None),
        P(),
        P("sp", "tp"),
        P("tp"),
        P("tp", "sp"),
        P("tp", "sp"),
        P("sp", "tp"),
    )
    out_specs = P("sp", "tp")
    return jax.shard_map(
        per_device, mesh=mesh, in_specs=in_specs, out_specs=out_specs, check_vma=False
    )
```

time: 734 us -> 527 us (0.72)
  the two profiles are of different devices: /device:TPU:1 before, /device:TPU:2 now
where the time goes in v1:
time: 527 us; the launch traced here: 526 us
  waiting for transfers between devices  392 us (74%)
  Pallas kernels  65.1 us (12%)
  blocking collectives  27.9 us (5%)
  matrix products  18.5 us (4%)
  between operations  13.9 us (3%)
  other arithmetic  8.64 us (2%)
    reduce_scatter x1, waiting for transfers between devices, per_device(): lax.psum_scatter(jnp.dot(normed_all, both_weights, preferred_element_type...  108 us
    all_gather x1, waiting for transfers between devices, per_device(): normed_all = lax.all_gather(normed, 'sp', axis=0, tiled=True)  75.1 us
    reduce_scatter x1, waiting for transfers between devices, per_device(): lax.psum_scatter(jnp.dot(hidden_all, w_down, preferred_element_type=jnp.f...  74.3 us
    reduce_scatter x1, waiting for transfers between devices, per_device(): lax.psum_scatter(jnp.dot(attended_all, w_out, preferred_element_type=jnp....  73.9 us
    pallas_call x1, Pallas kernels, run_attention(): pl.pallas_call(attention_kernel, out_shape=(jax.ShapeDtypeStruct((16, 128...  65.1 us
    all_gather x1, waiting for transfers between devices, per_device(): hidden_all = lax.all_gather(hidden, 'tp', axis=0, tiled=True)  60.5 us
    psum x1, blocking collectives, per_device(): squares = lax.psum(jnp.sum(wide * wide, axis=1), 'tp')  27.9 us
  transfers between devices with their start and end apart: 5, of which 5 were waited for; matrix products, arithmetic and copies ran while one was open for 0% of the time, Pallas kernels for 0%

profile of v1, /device:TPU:2, one launch (start us, length us, event | category | flops | bytes accessed | tf_op | source)
XLA Modules:
  0.0 526.3 jit_solution(1723012879652398215)
XLA Ops:
  7.3 0.7 maximum_bitcast_fusion
  8.0 1.6 pad_maximum_fusion.message_ref
  9.6 65.1 %attention.1 = (bf16[16,128,512]{2,1,0:T(8,128)(2,1)}, bf16[512,1024]{1,0:T(8,128)(2,1)}, bf16[512,1024]{1,0:T(8,128)(2,1)}) custom-call(s32[1]{0:T(128)S(6)} %copy.13.offset_ref, bf16[16,48,128]{2,1,0:T(8,128)(2,1)} %pad_maximum_fusion.message_ref, bf16[1024,1024]{1,0:T(8,128)(2,1)} %cache_k_ref.1, bf16[1024,1024]{1,0:T(8,128)(2,1)} %cache_v_ref.1, ...), custom_call_target="tpu_custom_call" | custom-call | tf_op jit(solution)/shard_map/attention/pallas_call | solution.py:271
  74.8 4.2 convolution_convert_fusion.2
  79.0 0.0 reduce-scatter.4.cloned.1.call-update
  79.0 0.0 all-gather.3.cloned.1.call-start
  79.1 73.9 %reduce-scatter.4.cloned.1.call-done = bf16[128,512]{1,0:T(8,128)(2,1)} async-done(((bf16[2048,512]{1,0:T(8,128)(2,1)}), bf16[128,512]{1,0:T(8,128)(2,1)}) %reduce-scatter.4.cloned.1.call-update) | async-done | bytes 131088 | tf_op jit(solution)/shard_map/reduce_scatter | solution.py:327
  153.0 1.0 fusion.4
  154.0 27.9 %psum.7 = f32[128]{0:T(128)S(1)} all-reduce(f32[128]{0:T(128)S(1)} %fusion.4), channel_id=1, replica_groups=mesh['sp'=16,'tp'=16] {'tp'}, use_global_device_ids=true, to_apply=%region_2.0 | all-reduce | flops 128 | bytes 1024 | tf_op jit(solution)/shard_map/psum | solution.py:335
  182.0 1.7 fusion.6
  183.6 0.0 all-gather.3.cloned.1.call-update
  183.7 0.0 reduce-scatter.6.cloned.1.call-start
  183.7 75.1 %all-gather.3.cloned.1.call-done = bf16[2048,512]{1,0:T(8,128)(2,1)} async-done(((bf16[128,512]{1,0:T(8,128)(2,1)}), bf16[2048,512]{1,0:T(8,128)(2,1)}) %all-gather.3.cloned.1.call-update) | async-done | bytes 2097168 | tf_op jit(solution)/shard_map/all_gather | solution.py:340
  258.8 8.5 %convolution_convert_fusion = bf16[2048,2048]{1,0:T(8,128)(2,1)} fusion(bf16[2048,512]{1,0:T(8,128)(2,1)} %all-gather.3.cloned.1.call-done, bf16[512,1024]{1,0:T(8,128)(2,1)S(1)} %copy-done.4, bf16[512,1024]{1,0:T(8,128)(2,1)S(1)} %copy-done.3), kind=kOutput, calls=%fused_computation | convolution fusion | flops 4303355904 | bytes 12582912 | tf_op jit(solution)/shard_map/dot_general | solution.py:344
  267.3 0.0 all-gather.5.cloned.1.call-start
  267.3 108.1 %reduce-scatter.6.cloned.1.call-done = bf16[128,2048]{1,0:T(8,128)(2,1)} async-done(((bf16[2048,2048]{1,0:T(8,128)(2,1)}), bf16[128,2048]{1,0:T(8,128)(2,1)}) %reduce-scatter.6.cloned.1.call-update) | async-done | bytes 524304 | tf_op jit(solution)/shard_map/reduce_scatter | solution.py:343
  375.4 1.1 convert_element_type.47
  376.6 0.9 fusion.3
  377.4 0.0 all-gather.5.cloned.1.call-update
  377.4 0.0 reduce-scatter.8.cloned.1.call-start
  377.5 60.5 %all-gather.5.cloned.1.call-done = bf16[2048,1024]{1,0:T(8,128)(2,1)} async-done(((bf16[128,1024]{1,0:T(8,128)(2,1)}), bf16[2048,1024]{1,0:T(8,128)(2,1)}) %all-gather.5.cloned.1.call-update) | async-done | bytes 4194320 | tf_op jit(solution)/shard_map/all_gather | solution.py:350
  438.0 5.8 %convolution_convert_fusion.1 = bf16[2048,512]{1,0:T(8,128)(2,1)} fusion(bf16[2048,1024]{1,0:T(8,128)(2,1)} %all-gather.5.cloned.1.call-done, bf16[1024,512]{1,0:T(8,128)(2,1)S(1)} %copy-done), kind=kOutput, calls=%fused_computation.1 | convolution fusion | flops 2148532224 | bytes 7340032 | tf_op jit(solution)/shard_map/dot_general | solution.py:352
  443.9 74.3 %reduce-scatter.8.cloned.1.call-done = bf16[128,512]{1,0:T(8,128)(2,1)} async-done(((bf16[2048,512]{1,0:T(8,128)(2,1)}), bf16[128,512]{1,0:T(8,128)(2,1)}) %reduce-scatter.8.cloned.1.call-update) | async-done | bytes 131088 | tf_op jit(solution)/shard_map/reduce_scatter | solution.py:351
  518.2 1.6 fusion.7
  (20 shorter events, 0.1 us)
Async XLA Ops:
  6.5 431.5 %copy-start = (bf16[1024,512]{1,0:T(8,128)(2,1)S(1)}, bf16[1024,512]{1,0:T(8,128)(2,1)}, u32[]{:S(2)}) copy-start(bf16[1024,512]{1,0:T(8,128)(2,1)} %param.23) | copy-start | bytes 3145732
  6.5 146.5 %reduce-scatter.4.cloned.1.call-start = ((), (), s32[]{:S(2)}) async-start(), calls=%async_computation.3 | async-start | bytes 2228224 | tf_op jit(solution)/shard_map/reduce_scatter | solution.py:327
  9.6 65.1 %copy-start.6 = (bf16[512,512]{1,0:T(8,128)(2,1)S(1)}, bf16[512,512]{1,0:T(8,128)(2,1)}, u32[]{:S(2)}) copy-start(bf16[512,512]{1,0:T(8,128)(2,1)} %param.19) | copy-start | bytes 1572868
  74.8 4.3 copy-start.5
  79.0 74.0 %copy-start.1 = (bf16[128,512]{1,0:T(8,128)(2,1)S(1)}, bf16[128,512]{1,0:T(8,128)(2,1)}, u32[]{:S(2)}) copy-start(bf16[128,512]{1,0:T(8,128)(2,1)} %param.12) | copy-start | bytes 393220
  79.0 179.8 %copy-start.3 = (bf16[512,1024]{1,0:T(8,128)(2,1)S(1)}, bf16[512,1024]{1,0:T(8,128)(2,1)}, u32[]{:S(2)}) copy-start(bf16[512,1024]{1,0:T(8,128)(2,1)} %w_gate_ref.1) | copy-start | bytes 3145732
  79.0 179.8 %copy-start.4 = (bf16[512,1024]{1,0:T(8,128)(2,1)S(1)}, bf16[512,1024]{1,0:T(8,128)(2,1)}, u32[]{:S(2)}) copy-start(bf16[512,1024]{1,0:T(8,128)(2,1)} %w_up_ref.1) | copy-start | bytes 3145732
  79.0 179.8 %all-gather.3.cloned.1.call-start = ((), (), s32[]{:S(2)}) async-start(), calls=%async_computation.4 | async-start | bytes 2228224 | tf_op jit(solution)/shard_map/all_gather | solution.py:340
  183.7 191.8 %reduce-scatter.6.cloned.1.call-start = ((), (), s32[]{:S(2)}) async-start(), calls=%async_computation.5 | async-start | bytes 8912896 | tf_op jit(solution)/shard_map/reduce_scatter | solution.py:343
  267.3 170.7 %all-gather.5.cloned.1.call-start = ((), (), s32[]{:S(2)}) async-start(), calls=%async_computation.6 | async-start | bytes 4456448 | tf_op jit(solution)/shard_map/all_gather | solution.py:350
  377.4 140.7 %reduce-scatter.8.cloned.1.call-start = ((), (), s32[]{:S(2)}) async-start(), calls=%async_computation.7 | async-start | bytes 2228224 | tf_op jit(solution)/shard_map/reduce_scatter | solution.py:351
  443.9 74.3 %copy-start.2 = (bf16[128,512]{1,0:T(8,128)(2,1)S(1)}, bf16[128,512]{1,0:T(8,128)(2,1)}, u32[]{:S(2)}) copy-start(bf16[128,512]{1,0:T(8,128)(2,1)} %reduce-scatter.4.cloned.1.call-done) | copy-start | bytes 393220
Sparse Core Ops, SparseCore 0:
  79.1 73.8 reduce-scatter.3
  183.8 74.9 all-gather.2
  267.4 107.9 reduce-scatter.5
  378.0 59.9 all-gather.4
  444.0 74.0 reduce-scatter.7

commit v2 on v1

--- a/solution.py
+++ b/solution.py
@@ -302,6 +302,327 @@
     )(offset, message, cache_keys, cache_values, w_gate, w_up)
 
 
+def scatter_z(product, total, sent, got, cross_send, cross_recv, send_sem, recv_sem, cross_sem):
+    sp, tp = here()
+    z, low = sp // 2, sp % 2
+    neighbours = (((sp + 2) % 16, tp), ((sp + 14) % 16, tp))
+    other = (sp + 1 - 2 * low, tp)
+
+    def hop(way, step, b):
+        return remote(
+            sent.at[way, step, b],
+            got.at[way, step, b],
+            send_sem.at[way * 8 + step * 2 + b],
+            recv_sem.at[way * 8 + step * 2 + b],
+            neighbours[way],
+        )
+
+    far = product((z + 4) % 8)
+    for way in range(2):
+        sent[way, 0, way] = far[way * 128 : way * 128 + 128].astype(BF)
+        hop(way, 0, way).start()
+    for step in range(1, 4):
+        distance = 4 - step
+        for way in range(2):
+            part = product((z + (distance if way == 0 else 8 - distance)) % 8)
+            for b in (1 - way, way):
+                piece = part[b * 128 : b * 128 + 128]
+                if step > 1 or b == way:
+                    hop(way, step - 1, b).wait_recv()
+                    piece = piece + got[way, step - 1, b].astype(F32)
+                sent[way, step, b] = piece.astype(BF)
+                hop(way, step, b).start()
+    total[...] = product(z).reshape(2, 128, 512)
+    for way in range(2):
+        for b in range(2):
+            hop(way, 3, b).wait_recv()
+            total[b] = total[b] + got[way, 3, b].astype(F32)
+    cross_send[...] = total[1 - low].astype(BF)
+    cross = remote(cross_send, cross_recv, cross_sem.at[0], cross_sem.at[1], other)
+    cross.start()
+    for way in range(2):
+        hop(way, 0, way).wait_send()
+        for step in range(1, 4):
+            for b in range(2):
+                hop(way, step, b).wait_send()
+    cross.wait()
+    return total[low] + cross_recv[...].astype(F32)
+
+
+def gather_z(own, blocks, paired, send_sem, recv_sem, cross_sem, pair_send, pair_recv):
+    sp, tp = here()
+    z, low = sp // 2, sp % 2
+    core = tp % 2
+    neighbours = (((sp + 2) % 16, tp), ((sp + 14) % 16, tp))
+    other = (sp + 1 - 2 * low, tp)
+    sibling = (sp, tp + 1 - 2 * core)
+
+    def hop(way, distance, place, b):
+        block = blocks.at[place, b]
+        index = way * 10 + distance * 2 + b
+        return remote(block, block, send_sem.at[index], recv_sem.at[index], neighbours[way])
+
+    def pass_on(place, b, offset):
+        @pl.when(b == 1 - core)
+        def _():
+            remote(blocks.at[place, b], paired.at[place], pair_send.at[offset], pair_recv.at[offset], sibling).start()
+
+    def from_way(way, distance):
+        return (z + (8 - distance if way == 0 else distance)) % 8
+
+    blocks[z, low] = own[...]
+    cross = remote(own, blocks.at[z, low], cross_sem.at[0], cross_sem.at[1], other)
+    cross.start()
+    for way in range(2):
+        hop(way, 1, z, low).start()
+    pass_on(z, low, 0)
+    came = blocks.at[z, 1 - low]
+    remote(own, came, cross_sem.at[0], cross_sem.at[1], other).wait_recv()
+    for way in range(2):
+        hop(way, 1, z, 1 - low).start()
+    pass_on(z, 1 - low, 0)
+    for distance in range(1, 4):
+        for b in (low, 1 - low):
+            for way in range(2):
+                place = from_way(way, distance)
+                hop(way, distance, place, b).wait_recv()
+                if distance < 3:
+                    hop(way, distance + 1, place, b).start()
+                else:
+
+                    @pl.when(b == way)
+                    def _():
+                        hop(way, 4, place, b).start()
+
+                pass_on(place, b, distance if way == 0 else 8 - distance)
+    for way in range(2):
+        place = (z + 4) % 8
+        hop(way, 4, place, way).wait_recv()
+        pass_on(place, way, 4)
+    cross.wait_send()
+    for way in range(2):
+        for distance in range(1, 4):
+            for b in range(2):
+                hop(way, distance, z, b).wait_send()
+        hop(way, 4, z, way).wait_send()
+
+    def settle(offset, _):
+        place = (z + 8 - offset) % 8
+        remote(blocks.at[place, 0], paired.at[place], pair_send.at[offset], pair_recv.at[offset], sibling).wait()
+        return 0
+
+    lax.fori_loop(0, 8, settle, 0)
+
+
+def tail_kernel(
+    attended_ref,
+    w_out_ref,
+    residual_ref,
+    gain_ref,
+    w_gate_ref,
+    w_up_ref,
+    other_gate_ref,
+    other_up_ref,
+    w_down_ref,
+    out_ref,
+    stream,
+    total,
+    sent_a,
+    got_a,
+    sent_d,
+    got_d,
+    cross_a,
+    cross_d,
+    squares,
+    own_squares,
+    own_normed,
+    normed,
+    paired,
+    x_sent,
+    x_got,
+    y_sent,
+    y_got,
+    own_hidden,
+    hidden,
+    za_send,
+    za_recv,
+    zd_send,
+    zd_recv,
+    ca_sem,
+    cd_sem,
+    cn_sem,
+    sq_send,
+    sq_recv,
+    zn_send,
+    zn_recv,
+    pn_send,
+    pn_recv,
+    x_send,
+    x_recv,
+    y_sem,
+    ag_send,
+    ag_recv,
+    fw_send,
+    fw_recv,
+):
+    sp, tp = here()
+    core, chip = tp % 2, tp // 2
+    high, x = chip // 4, chip % 4
+    greet(
+        [((sp + 2) % 16, tp), ((sp + 14) % 16, tp), (sp + 1 - 2 * (sp % 2), tp)]
+        + [(sp, (tp + j) % 16) for j in range(1, 16)]
+    )
+    attended = attended_ref
+    attn_out = scatter_z(
+        lambda place: jnp.dot(attended[place], w_out_ref[...], preferred_element_type=F32),
+        total, sent_a, got_a, cross_a.at[0], cross_a.at[1], za_send, za_recv, ca_sem,
+    )
+    stream[...] = (residual_ref[...].astype(F32) + attn_out).astype(BF)
+    wide = stream[...].astype(F32)
+    square = wide * wide
+    square = square[:, :128] + square[:, 128:256] + square[:, 256:384] + square[:, 384:]
+    own_squares[...] = jnp.broadcast_to(jnp.sum(square.T, axis=0, keepdims=True), (8, 128))
+    squares[tp] = own_squares[...]
+
+    def tell(j, _):
+        remote(own_squares, squares.at[tp], sq_send.at[j], sq_recv.at[j], (sp, (tp + j) % 16)).start()
+        return 0
+
+    lax.fori_loop(1, 16, tell, 0)
+
+    def told(j, _):
+        block = squares.at[(tp + 16 - j) % 16]
+        remote(own_squares, block, sq_send.at[j], sq_recv.at[j], (sp, (tp + j) % 16)).wait()
+        return 0
+
+    lax.fori_loop(1, 16, told, 0)
+    summed = jnp.sum(squares[...], axis=0)
+    scale = lax.rsqrt(jnp.broadcast_to(summed[0:1], (128, 128)).T / D + EPS)
+    scale = jnp.concatenate([scale] * 4, axis=1)
+    own_normed[...] = (stream[...].astype(F32) * scale * gain_ref[...]).astype(BF)
+    gather_z(own_normed, normed, paired, zn_send, zn_recv, cn_sem, pn_send, pn_recv)
+
+    def part(upper, column, up):
+        place = upper * 4 + (x + column) % 4
+        mine, others = (w_up_ref, other_up_ref) if up else (w_gate_ref, other_gate_ref)
+        return jnp.dot(normed[place, core], mine[...], preferred_element_type=F32) + jnp.dot(
+            paired[place], others[...], preferred_element_type=F32
+        )
+
+    neighbours = (
+        (sp, (high * 4 + (x + 1) % 4) * 2 + core),
+        (sp, (high * 4 + (x + 3) % 4) * 2 + core),
+    )
+
+    def hop(turn, which):
+        index = turn * 6 + which
+        return remote(
+            x_sent.at[index], x_got.at[index], x_send.at[index], x_recv.at[index], neighbours[which // 3]
+        )
+
+    def post(turn, which, value):
+        x_sent[turn * 6 + which] = value.astype(BF)
+        hop(turn, which).start()
+
+    def arrived(turn, which):
+        hop(turn, which).wait_recv()
+        return x_got[turn * 6 + which].astype(F32)
+
+    uppers = (1 - high, high)
+
+    def open_turn(turn):
+        upper = uppers[turn]
+        post(turn, 0, part(upper, 2, False))
+        post(turn, 3, part(upper, 2, True))
+        post(turn, 2, part(upper, 1, True))
+        post(turn, 5, part(upper, 3, False))
+
+    def second_hop(turn):
+        upper = uppers[turn]
+        gate = part(upper, 1, False)
+        post(turn, 1, gate + arrived(turn, 0))
+        up = part(upper, 3, True)
+        post(turn, 4, up + arrived(turn, 3))
+
+    def close_turn(turn, up):
+        value = part(uppers[turn], 0, up)
+        first, second = (2, 4) if up else (5, 1)
+        return value + arrived(turn, first) + arrived(turn, second)
+
+    opposite = (sp, ((1 - high) * 4 + x) * 2 + core)
+
+    def over(index):
+        return remote(y_sent.at[index], y_got.at[index], y_sem.at[index], y_sem.at[2 + index], opposite)
+
+    open_turn(0)
+    second_hop(0)
+    open_turn(1)
+    for index in range(2):
+        y_sent[index] = close_turn(0, index == 1).astype(BF)
+        over(index).start()
+    second_hop(1)
+    gate = close_turn(1, False)
+    up = close_turn(1, True)
+    over(0).wait()
+    gate = gate + y_got[0].astype(F32)
+    over(1).wait()
+    up = up + y_got[1].astype(F32)
+    own_hidden[...] = (gate / (1.0 + jnp.exp(-gate)) * up).astype(BF)
+    gather_tp(own_hidden, hidden, ag_send, ag_recv, fw_send, fw_recv)
+    for turn in range(2):
+        for which in range(6):
+            hop(turn, which).wait_send()
+
+    def down(place):
+        first = jnp.dot(hidden[2 * place], w_down_ref[...], preferred_element_type=F32)
+        second = jnp.dot(hidden[2 * place + 1], w_down_ref[...], preferred_element_type=F32)
+        return jnp.concatenate([first, second], 0)
+
+    added = scatter_z(down, total, sent_d, got_d, cross_d.at[0], cross_d.at[1], zd_send, zd_recv, cd_sem)
+    out_ref[...] = (stream[...].astype(F32) + added).astype(BF)
+
+
+def run_tail(attended, w_out, residual, gain, w_gate, w_up, other_gate, other_up, w_down):
+    hop = VM((2, 4, 2, 128, 512), BF)
+    return pl.pallas_call(
+        tail_kernel,
+        out_shape=jax.ShapeDtypeStruct((128, 512), BF),
+        in_specs=in_vmem(9),
+        out_specs=in_vmem(1)[0],
+        scratch_shapes=[
+            VM((128, 512), BF),
+            VM((2, 128, 512), F32),
+            hop,
+            hop,
+            hop,
+            hop,
+            VM((2, 128, 512), BF),
+            VM((2, 128, 512), BF),
+            VM((16, 8, 128), F32),
+            VM((8, 128), F32),
+            VM((128, 512), BF),
+            VM((8, 2, 128, 512), BF),
+            VM((8, 128, 512), BF),
+            VM((12, 128, 1024), BF),
+            VM((12, 128, 1024), BF),
+            VM((2, 128, 1024), BF),
+            VM((2, 128, 1024), BF),
+            VM((128, 1024), BF),
+            VM((16, 128, 1024), BF),
+        ]
+        + [DMA((16,))] * 4
+        + [DMA((2,))] * 3
+        + [DMA((16,))] * 2
+        + [DMA((20,))] * 2
+        + [DMA((8,))] * 2
+        + [DMA((12,))] * 2
+        + [DMA((4,))]
+        + [DMA((8,))] * 4,
+        compiler_params=params(1),
+        name="tail",
+    )(attended, w_out, residual, gain, w_gate, w_up, other_gate, other_up, w_down)
+
+
 def per_device(
     residual,
     queries,
@@ -323,38 +644,18 @@
     attended_all, other_gate, other_up = run_attention(
         offset, message, cache_keys, cache_values, w_gate, w_up
     )
-    attended_all = attended_all.reshape(2048, 512)
-    attn_out = lax.psum_scatter(
-        jnp.dot(attended_all, w_out, preferred_element_type=jnp.float32).astype(jnp.bfloat16),
-        "sp",
-        scatter_dimension=0,
-        tiled=True,
-    ).astype(jnp.float32)
-    stream = (residual.astype(jnp.float32) + attn_out).astype(jnp.bfloat16)
-    wide = stream.astype(jnp.float32)
-    squares = lax.psum(jnp.sum(wide * wide, axis=1), "tp")
-    scale_rows = lax.rsqrt(squares / D + 1e-06)
-    normed = (wide * scale_rows[:, None] * norm_gain.astype(jnp.float32)[None, :]).astype(
-        jnp.bfloat16
-    )
-    normed_all = lax.all_gather(normed, "sp", axis=0, tiled=True)
-    both_weights = jnp.concatenate([w_gate, w_up], 1)
-    width = w_gate.shape[1]
-    both = lax.psum_scatter(
-        jnp.dot(normed_all, both_weights, preferred_element_type=jnp.float32).astype(jnp.bfloat16),
-        "tp",
-        scatter_dimension=0,
-        tiled=True,
-    ).astype(jnp.float32)
-    hidden = (jax.nn.silu(both[:, :width]) * both[:, width:]).astype(jnp.bfloat16)
-    hidden_all = lax.all_gather(hidden, "tp", axis=0, tiled=True)
-    down = lax.psum_scatter(
-        jnp.dot(hidden_all, w_down, preferred_element_type=jnp.float32).astype(jnp.bfloat16),
-        "sp",
-        scatter_dimension=0,
-        tiled=True,
-    ).astype(jnp.float32)
-    return (wide + down).astype(jnp.bfloat16)
+    gain = norm_gain.astype(F32).reshape(1, 512)
+    return run_tail(
+        attended_all.reshape(8, 256, 512),
+        w_out,
+        residual,
+        gain,
+        w_gate,
+        w_up,
+        other_gate,
+        other_up,
+        w_down,
+    )
 
 
 def solution(mesh):

time: 527 us -> 244 us (0.46)
  the two profiles are of different devices: /device:TPU:2 before, /device:TPU:1 now
where the time goes in v2:
time: 244 us; the launch traced here: 240 us
  Pallas kernels  235 us (96%)
  other arithmetic  2.9 us (1%)
    pallas_call x1, Pallas kernels, run_tail(): pl.pallas_call(tail_kernel, out_shape=jax.ShapeDtypeStruct((128, 512), BF...  167 us
    pallas_call x1, Pallas kernels, run_attention(): pl.pallas_call(attention_kernel, out_shape=(jax.ShapeDtypeStruct((16, 128...  68.7 us

profile of v2, /device:TPU:1, one launch (start us, length us, event | category | flops | bytes accessed | tf_op | source)
XLA Modules:
  0.0 240.4 jit_solution(2206471521129198334)
XLA Ops:
  0.0 0.7 maximum_bitcast_fusion
  0.8 1.6 pad_maximum_fusion.message_ref
  3.0 0.0 copy-start
  3.0 68.7 %attention.1 = (bf16[16,128,512]{2,1,0:T(8,128)(2,1)}, bf16[512,1024]{1,0:T(8,128)(2,1)}, bf16[512,1024]{1,0:T(8,128)(2,1)}) custom-call(s32[1]{0:T(128)S(6)} %copy.14.offset_ref, bf16[16,48,128]{2,1,0:T(8,128)(2,1)} %pad_maximum_fusion.message_ref, bf16[1024,1024]{1,0:T(8,128)(2,1)} %cache_k_ref.1, bf16[1024,1024]{1,0:T(8,128)(2,1)} %cache_v_ref.1, ...), custom_call_target="tpu_custom_call" | custom-call | tf_op jit(solution)/shard_map/attention/pallas_call | solution.py:271
  71.7 0.0 copy-done
  71.7 0.6 reshape.27
  72.3 166.5 %tail.1 = bf16[128,512]{1,0:T(8,128)(2,1)} custom-call(bf16[8,256,512]{2,1,0:T(8,128)(2,1)} %bitcast.14, bf16[512,512]{1,0:T(8,128)(2,1)} %w_out_ref.1, bf16[128,512]{1,0:T(8,128)(2,1)} %residual_ref.1, f32[1,512]{1,0:T(1,128)} %bitcast.19, bf16[512,1024]{1,0:T(8,128)(2,1)} %w_gate_ref.3, bf16[512,1024]{1,0:T(8,128)(2,1)} %w_up_ref.3, ...), custom_call_target="tpu_custom_call" | custom-call | tf_op jit(solution)/shard_map/tail/pallas_call | solution.py:587
  238.8 1.6 copy.15
  (1 shorter events, 0.0 us)
Async XLA Ops:
  3.0 68.7 %copy-start = (bf16[512]{0:T(512)(128)(2,1)S(1)}, bf16[512]{0:T(512)(128)(2,1)}, u32[]{:S(2)}) copy-start(bf16[512]{0:T(512)(128)(2,1)} %param.20) | copy-start | bytes 3076

commit v3 on v1

v3 whole, which is shorter than its diff:
```python
import functools

import jax
import jax.numpy as jnp
from jax import lax
from jax.experimental import pallas as pl
from jax.experimental.pallas import tpu as pltpu
from jax.sharding import PartitionSpec as P

D = 8192
H = 64
KV = 8
HD = 128
EPS = 1e-6
BF = jnp.bfloat16
F32 = jnp.float32
MESH = pl.DeviceIdType.MESH
VM = pltpu.VMEM
DMA = pltpu.SemaphoreType.DMA
SCORE_SCALE = 1.4426950408889634 / HD**0.5
LOWEST = -1e30
VMEM_LIMIT = 56 * 2**20


def remote(src, dst, send, recv, device):
    return pltpu.make_async_remote_copy(
        src_ref=src,
        dst_ref=dst,
        send_sem=send,
        recv_sem=recv,
        device_id=device,
        device_id_type=MESH,
    )


def tp_of(place, x):
    return ((place // 2) * 4 + x) * 2 + place % 2


def greet(devices):
    barrier = pltpu.get_barrier_semaphore()
    for device in devices:
        pl.semaphore_signal(barrier, inc=1, device_id=device, device_id_type=MESH)
    pl.semaphore_wait(barrier, len(devices))


class Spread:
    def __init__(self, source, buffer, sems, first, local=True):
        sp, tp = lax.axis_index("sp"), lax.axis_index("tp")
        high, x, core = tp // 8, (tp // 2) % 4, tp % 2
        self.sems = sems
        self.first = first
        self.buffer = buffer
        self.sibling = (sp, tp + 1 - 2 * core)
        opposite = (sp, (tp + 8) % 16)
        mine = buffer.at[high * 2 + core]
        self.local = pltpu.make_async_copy(source, mine, sems.at[first]) if local else None
        self.pair = remote(source, mine, sems.at[first + 1], sems.at[first + 2], self.sibling)
        self.over = remote(source, mine, sems.at[first + 3], sems.at[first + 4], opposite)
        across = buffer.at[(1 - high) * 2 + core]
        self.passed = remote(across, across, sems.at[first + 5], sems.at[first + 6], self.sibling)

    def keep(self):
        self.local.start()

    def send(self):
        self.over.start()
        self.pair.start()

    def forward(self):
        self.over.wait_recv()
        self.passed.start()

    def finish(self):
        if self.local is not None:
            self.local.wait()
        self.pair.wait()
        self.over.wait_send()
        self.passed.wait()


def gather_x(own, blocks, send_sem, recv_sem):
    sp, tp = lax.axis_index("sp"), lax.axis_index("tp")
    x, place = (tp // 2) % 4, (tp // 8) * 2 + tp % 2
    copies = [
        remote(own, blocks.at[x], send_sem.at[k], recv_sem.at[k], (sp, tp_of(place, (x + k) % 4)))
        for k in (1, 3, 2)
    ]
    for copy in copies:
        copy.start()
    blocks[x] = own[...]
    for copy in copies:
        copy.wait()


def scatter_z(product, sent, got, cross_send, cross_recv, send_sem, recv_sem, cross_sem):
    sp, tp = lax.axis_index("sp"), lax.axis_index("tp")
    z, low = sp // 2, sp % 2
    neighbours = (((sp + 2) % 16, tp), ((sp + 14) % 16, tp))
    other = (sp + 1 - 2 * low, tp)

    def hop(way, step, r):
        index = way * 8 + step * 2 + r
        return remote(
            sent.at[way, step, r], got.at[way, step, r], send_sem.at[index], recv_sem.at[index], neighbours[way]
        )

    def split(place):
        part = product(place)
        return jnp.where(low == 0, part[32:], part[:32]), jnp.where(low == 0, part[:32], part[32:])

    far = split((z + 4) % 8)
    for way in range(2):
        sent[way, 0, way] = far[way].astype(BF)
        hop(way, 0, way).start()
    for step in range(1, 4):
        parts = [split((z + 4 - step) % 8), split((z + 4 + step) % 8)]
        for r in range(2):
            for way in range(2):
                piece = parts[way][r]
                if step > 1 or r == way:
                    hop(way, step - 1, r).wait_recv()
                    piece = piece + got[way, step - 1, r].astype(F32)
                sent[way, step, r] = piece.astype(BF)
                hop(way, step, r).start()
    away, mine = split(z)
    for way in range(2):
        hop(way, 3, 0).wait_recv()
        away = away + got[way, 3, 0].astype(F32)
    cross_send[...] = away.astype(BF)
    cross = remote(cross_send, cross_recv, cross_sem.at[0], cross_sem.at[1], other)
    cross.start()
    for way in range(2):
        hop(way, 3, 1).wait_recv()
        mine = mine + got[way, 3, 1].astype(F32)
    for way in range(2):
        hop(way, 0, way).wait_send()
        for step in range(1, 4):
            for r in range(2):
                hop(way, step, r).wait_send()
    cross.wait()
    return mine + cross_recv[...].astype(F32)


def gather_z(own, blocks, send_sem, recv_sem, cross_sem):
    sp, tp = lax.axis_index("sp"), lax.axis_index("tp")
    z, low = sp // 2, sp % 2
    neighbours = (((sp + 2) % 16, tp), ((sp + 14) % 16, tp))
    other = (sp + 1 - 2 * low, tp)

    def hop(way, distance, place, r):
        block = blocks.at[place, low if r == 0 else 1 - low]
        index = way * 10 + distance * 2 + r
        return remote(block, block, send_sem.at[index], recv_sem.at[index], neighbours[way])

    blocks[z, low] = own[...]
    cross = remote(own, blocks.at[z, low], cross_sem.at[0], cross_sem.at[1], other)
    cross.start()
    for way in range(2):
        hop(way, 1, z, 0).start()
    remote(own, blocks.at[z, 1 - low], cross_sem.at[0], cross_sem.at[1], other).wait_recv()
    for way in range(2):
        hop(way, 1, z, 1).start()
    for distance in range(1, 4):
        for r in range(2):
            for way in range(2):
                place = (z + (8 - distance if way == 0 else distance)) % 8
                hop(way, distance, place, r).wait_recv()
                if distance < 3 or r == way:
                    hop(way, distance + 1, place, r).start()
    for way in range(2):
        hop(way, 4, (z + 4) % 8, way).wait_recv()
    cross.wait_send()
    for way in range(2):
        for distance in range(1, 4):
            for r in range(2):
                hop(way, distance, z, r).wait_send()
        hop(way, 4, z, way).wait_send()


def block_kernel(
    offset_ref,
    message_ref,
    residual_ref,
    gain_ref,
    cache_k_ref,
    cache_v_ref,
    w_out_ref,
    w_gate_ref,
    w_up_ref,
    w_down_ref,
    out_ref,
    received,
    keys,
    own_vals,
    vals_t,
    new_keys,
    new_vals_t,
    own_queries,
    queries,
    out_send,
    out_recv,
    stat_send,
    stat_recv,
    own_attended,
    attended,
    w_out,
    w_gate,
    w_up,
    w_down,
    gains,
    residuals,
    stream,
    sent_a,
    got_a,
    sent_d,
    got_d,
    cross_a,
    cross_d,
    own_squares,
    squares,
    own_normed,
    normed,
    x_sent,
    x_got,
    own_hidden,
    hidden,
    own_out,
    a2a_send,
    a2a_recv,
    spread_sem,
    small_sem,
    q_send,
    q_recv,
    o_send,
    o_recv,
    st_send,
    st_recv,
    aa_send,
    aa_recv,
    za_send,
    za_recv,
    sq_send,
    sq_recv,
    zn_send,
    zn_recv,
    x_send,
    x_recv,
    ah_send,
    ah_recv,
    zd_send,
    zd_recv,
    cross_sem,
    back_sem,
):
    sp, tp = lax.axis_index("sp"), lax.axis_index("tp")
    high, x, core = tp // 8, (tp // 2) % 4, tp % 2
    place = high * 2 + core
    greet([((sp + j) % 16, tp) for j in range(1, 16)] + [(sp, (tp + j) % 16) for j in range(1, 16)])

    def exchange(j, _):
        target = (sp + j) % 16
        remote(message_ref.at[target], received.at[sp], a2a_send.at[j], a2a_recv.at[j], (target, tp)).start()
        return 0

    lax.fori_loop(1, 16, exchange, 0)
    columns = pl.ds(pl.multiple_of((sp // 2) * HD, HD), HD)
    spread_k = Spread(cache_k_ref.at[:, columns], keys, spread_sem, 0)
    spread_v = Spread(vals_t.at[place], vals_t, spread_sem, 7, local=False)
    spread_o = Spread(w_out_ref, w_out, spread_sem, 14)
    spread_g = Spread(w_gate_ref, w_gate, spread_sem, 21)
    spread_u = Spread(w_up_ref, w_up, spread_sem, 28)
    spread_d = Spread(w_down_ref, w_down, spread_sem, 35)
    load_v = pltpu.make_async_copy(cache_v_ref.at[:, columns], own_vals, small_sem.at[0])
    load_v.start()
    spread_k.keep()
    spread_k.send()
    received[sp] = message_ref[sp]
    load_v.wait()
    for piece in range(4):
        rows = own_vals[piece * 256 : piece * 256 + 256, :].astype(F32)
        vals_t[place, :, piece * 256 : piece * 256 + 256] = rows.T.astype(BF)
    spread_v.send()
    for spread in (spread_o, spread_g, spread_u, spread_d):
        spread.keep()

    def arrived(j, _):
        block = received.at[(sp + 16 - j) % 16]
        remote(block, block, a2a_send.at[j], a2a_recv.at[j], (sp, tp)).wait()
        return 0

    lax.fori_loop(1, 16, arrived, 0)
    own_queries[...] = received[:, :32, :].reshape(4, 128, HD)
    queries[x, place] = own_queries[place]

    def ask(i, _):
        target = tp_of(i % 4, (x + i // 4) % 4)
        j = (target - tp + 16) % 16

        @pl.when(j > 0)
        def _():
            remote(own_queries.at[i % 4], queries.at[x, place], q_send.at[j], q_recv.at[j], (sp, target)).start()

        return 0

    lax.fori_loop(0, 16, ask, 0)
    fresh = received[:, 32:, :].astype(F32).reshape(16, 2, 8, HD)
    new_keys[place] = fresh[:, 0].reshape(HD, HD).astype(BF)
    new_vals_t[place] = fresh[:, 1].reshape(HD, HD).T.astype(BF)

    def quad(i):
        peer = (place + i) % 4
        return (sp, tp_of(peer, x))

    def to_quad(i, kind, src, dst):
        index = 1 + kind * 6 + (i - 1) * 2
        return remote(src, dst, small_sem.at[index], small_sem.at[index + 1], quad(i))

    smalls = []
    for i in range(1, 4):
        peer = (place + i) % 4
        rows = pl.ds(pl.multiple_of(peer * 32, 32), 32)
        smalls.append(to_quad(i, 0, new_keys.at[place], new_keys.at[place]))
        smalls.append(to_quad(i, 1, new_vals_t.at[place], new_vals_t.at[place]))
        smalls.append(to_quad(i, 2, residual_ref.at[rows], residuals.at[place]))
        smalls.append(to_quad(i, 3, gain_ref, gains.at[place]))
    for copy in smalls:
        copy.start()
    residuals[place] = residual_ref[pl.ds(pl.multiple_of(place * 32, 32), 32)]
    gains[place] = gain_ref[...]
    spread_k.forward()
    spread_v.forward()
    spread_k.finish()
    spread_v.finish()
    for copy in smalls:
        copy.wait()
    spread_o.send()
    spread_g.send()

    def attend(k, _):
        asker = (x + 4 - k) % 4
        for source in range(4):
            j = (tp - tp_of(source, asker) + 16) % 16

            @pl.when(j > 0)
            def _():
                block = queries.at[asker, source]
                remote(block, block, q_send.at[j], q_recv.at[j], (sp, tp)).wait_recv()

        q = queries[asker].reshape(512, HD)
        top = jnp.full((1, 512), LOWEST, F32)
        total = jnp.zeros((1, 512), F32)
        summed = jnp.zeros((HD, 512), F32)
        lane = lax.broadcasted_iota(jnp.int32, (128, 512), 1)
        token = ((lane // 256) * 4 + asker) * 256 + ((lane // 128) % 2) * 128
        token = token + place * 32 + ((lane // 32) % 4) * 8 + lane % 8
        ahead = lax.broadcasted_iota(jnp.int32, (128, 512), 0) - token
        for chunk in range(9):
            held, first = chunk // 2, (chunk % 2) * 512
            if chunk < 8:
                block = keys[held, first : first + 512, :]
                block_t = vals_t[held, :, first : first + 512]
            else:
                block = new_keys[...].reshape(512, HD)
                block_t = jnp.concatenate([new_vals_t[i] for i in range(4)], 1)
            scores = lax.dot_general(block, q, (((1,), (1,)), ((), ())), preferred_element_type=F32)
            if chunk < 8:
                position = lax.broadcasted_iota(jnp.int32, (512, 512), 0)
                scores = jnp.where(position < offset_ref[0] - tp_of(held, x) * 1024 - first, scores, LOWEST)
            else:
                scores = jnp.concatenate(
                    [
                        jnp.where(ahead <= -tp_of(i, x) * 128, scores[i * 128 : i * 128 + 128], LOWEST)
                        for i in range(4)
                    ],
                    0,
                )
            higher = jnp.maximum(top, jnp.max(scores, axis=0, keepdims=True))
            weights = jnp.exp2((scores - higher) * SCORE_SCALE)
            factor = jnp.exp2((top - higher) * SCORE_SCALE)
            total = total * factor + jnp.sum(weights, axis=0, keepdims=True)
            summed = summed * factor + jnp.dot(block_t, weights.astype(BF), preferred_element_type=F32)
            top = higher
        out_send[k] = summed.astype(BF)
        stat_send[k] = jnp.concatenate([jnp.broadcast_to(top, (4, 512)), jnp.broadcast_to(total, (4, 512))], 0)

        @pl.when(k > 0)
        def _():
            target = (sp, tp_of(place, asker))
            remote(out_send.at[k], out_recv.at[k], o_send.at[k], o_recv.at[k], target).start()
            remote(stat_send.at[k], stat_recv.at[k], st_send.at[k], st_recv.at[k], target).start()

        return 0

    lax.fori_loop(0, 4, attend, 0)
    spread_o.forward()
    spread_u.send()

    def asked(j, _):
        remote(own_queries.at[0], queries.at[x, place], q_send.at[j], q_recv.at[j], (sp, tp)).wait_send()
        return 0

    lax.fori_loop(1, 16, asked, 0)

    def collect(k, _):
        remote(out_send.at[k], out_recv.at[k], o_send.at[k], o_recv.at[k], (sp, tp)).wait()
        remote(stat_send.at[k], stat_recv.at[k], st_send.at[k], st_recv.at[k], (sp, tp)).wait()
        return 0

    lax.fori_loop(1, 4, collect, 0)
    tops = [stat_send[0, 0:1, :]] + [stat_recv[k, 0:1, :] for k in range(1, 4)]
    highest = functools.reduce(jnp.maximum, tops)
    shares = [jnp.exp2((top - highest) * SCORE_SCALE) for top in tops]
    total = stat_send[0, 4:5, :] * shares[0]
    summed = out_send[0].astype(F32) * shares[0]
    for k in range(1, 4):
        total = total + stat_recv[k, 4:5, :] * shares[k]
        summed = summed + out_recv[k].astype(F32) * shares[k]
    mixed = (summed / total).T.reshape(16, 4, 8, HD)
    for h in range(4):
        own_attended[:, :, h * HD : (h + 1) * HD] = mixed[:, h].reshape(2, 64, HD).astype(BF)
    gather_x(own_attended, attended, aa_send, aa_recv)
    spread_o.finish()

    def project(z):
        rows = attended[z % 4, z // 4]
        return jnp.concatenate(
            [jnp.dot(rows, w_out[i], preferred_element_type=F32) for i in range(4)], 1
        )

    attn_out = scatter_z(
        project, sent_a, got_a, cross_a.at[0], cross_a.at[1], za_send, za_recv, cross_sem.at[pl.ds(0, 2)]
    )
    spread_g.forward()
    spread_u.forward()
    spread_d.send()
    own_residual = jnp.concatenate([residuals[i] for i in range(4)], 1)
    stream[...] = (own_residual.astype(F32) + attn_out).astype(BF)
    wide = stream[...].astype(F32)
    own_squares[...] = jnp.broadcast_to(jnp.sum(wide * wide, axis=1, keepdims=True), (32, 128))
    tells = [
        remote(own_squares, squares.at[k], sq_send.at[k], sq_recv.at[k], (sp, tp_of(place, (x + k) % 4)))
        for k in range(1, 4)
    ]
    for copy in tells:
        copy.start()
    for copy in tells:
        copy.wait()
    mean = (own_squares[...] + squares[1] + squares[2] + squares[3]) / D
    scale = jnp.concatenate([lax.rsqrt(mean + EPS)] * 16, 1)
    gain = jnp.concatenate([gains[i, 0:1, :] for i in range(4)], 1)
    own_normed[...] = (stream[...].astype(F32) * scale * gain).astype(BF)
    gather_z(own_normed, normed, zn_send, zn_recv, cross_sem.at[pl.ds(2, 2)])
    spread_d.forward()
    spread_g.finish()
    spread_u.finish()

    def part(column, up):
        rows = normed[pl.ds(2 * ((x + column) % 4), 2)].reshape(128, 2048)
        weight = w_up if up else w_gate
        return jnp.dot(rows, weight[...].reshape(2048, 1024), preferred_element_type=F32)

    neighbours = ((sp, tp_of(place, (x + 1) % 4)), (sp, tp_of(place, (x + 3) % 4)))

    def hop(which):
        return remote(
            x_sent.at[which], x_got.at[which], x_send.at[which], x_recv.at[which], neighbours[which // 3]
        )

    def post(which, value):
        x_sent[which] = value.astype(BF)
        hop(which).start()

    def came(which):
        hop(which).wait_recv()
        return x_got[which].astype(F32)

    post(0, part(2, False))
    post(3, part(2, True))
    post(2, part(1, True))
    post(5, part(3, False))
    second = part(1, False)
    post(1, second + came(0))
    second = part(3, True)
    post(4, second + came(3))
    gate = part(0, False)
    up = part(0, True)
    gate = gate + came(5) + came(1)
    up = up + came(2) + came(4)
    own_hidden[...] = (gate / (1.0 + jnp.exp(-gate)) * up).astype(BF).reshape(2, 64, 1024)
    gather_x(own_hidden, hidden, ah_send, ah_recv)
    spread_d.finish()
    for which in range(6):
        hop(which).wait_send()

    def down(z):
        rows = hidden[z // 2, z % 2]
        return jnp.concatenate(
            [jnp.dot(rows, w_down[i], preferred_element_type=F32) for i in range(4)], 1
        )

    added = scatter_z(
        down, sent_d, got_d, cross_d.at[0], cross_d.at[1], zd_send, zd_recv, cross_sem.at[pl.ds(4, 2)]
    )
    result = (stream[...].astype(F32) + added).astype(BF)
    for i in range(4):
        own_out[i] = result[:, i * 512 : i * 512 + 512]
    mine = pl.ds(pl.multiple_of(place * 32, 32), 32)
    backs = [
        remote(own_out.at[(place + i) % 4], out_ref.at[mine], back_sem.at[2 * i], back_sem.at[2 * i + 1], quad(i))
        for i in range(1, 4)
    ]
    for copy in backs:
        copy.start()
    out_ref[mine] = own_out[place]
    for copy in backs:
        copy.wait()


def run_block(offset, message, residual, gain, cache_keys, cache_values, w_out, w_gate, w_up, w_down):
    hop = VM((2, 4, 2, 32, 2048), BF)
    vmem = pl.BlockSpec(memory_space=pltpu.VMEM)
    return pl.pallas_call(
        block_kernel,
        out_shape=jax.ShapeDtypeStruct((128, 512), BF),
        in_specs=[pl.BlockSpec(memory_space=pltpu.SMEM)] + [vmem] * 3 + [pl.BlockSpec(memory_space=pl.ANY)] * 6,
        out_specs=vmem,
        scratch_shapes=[
            VM((16, 48, HD), BF),
            VM((4, 1024, HD), BF),
            VM((1024, HD), BF),
            VM((4, HD, 1024), BF),
            VM((4, 128, HD), BF),
            VM((4, HD, 128), BF),
            VM((4, 128, HD), BF),
            VM((4, 4, 128, HD), BF),
            VM((4, HD, 512), BF),
            VM((4, HD, 512), BF),
            VM((4, 8, 512), F32),
            VM((4, 8, 512), F32),
            VM((2, 64, 512), BF),
            VM((4, 2, 64, 512), BF),
            VM((4, 512, 512), BF),
            VM((4, 512, 1024), BF),
            VM((4, 512, 1024), BF),
            VM((4, 1024, 512), BF),
            VM((4, 8, 512), F32),
            VM((4, 32, 512), BF),
            VM((32, 2048), BF),
            hop,
            hop,
            hop,
            hop,
            VM((2, 32, 2048), BF),
            VM((2, 32, 2048), BF),
            VM((32, 128), F32),
            VM((4, 32, 128), F32),
            VM((32, 2048), BF),
            VM((8, 2, 32, 2048), BF),
            VM((6, 128, 1024), BF),
            VM((6, 128, 1024), BF),
            VM((2, 64, 1024), BF),
            VM((4, 2, 64, 1024), BF),
            VM((4, 32, 512), BF),
        ]
        + [DMA((16,))] * 2
        + [DMA((42,)), DMA((25,))]
        + [DMA((16,))] * 2
        + [DMA((4,))] * 6
        + [DMA((16,))] * 2
        + [DMA((4,))] * 2
        + [DMA((20,))] * 2
        + [DMA((6,))] * 2
        + [DMA((4,))] * 2
        + [DMA((16,))] * 2
        + [DMA((6,)), DMA((8,))],
        compiler_params=pltpu.CompilerParams(
            collective_id=0, has_side_effects=True, vmem_limit_bytes=VMEM_LIMIT
        ),
        name="block",
    )(offset, message, residual, gain, cache_keys, cache_values, w_out, w_gate, w_up, w_down)


def per_device(
    residual,
    queries,
    keys,
    values,
    cache_keys,
    cache_values,
    offset,
    w_out,
    norm_gain,
    w_gate,
    w_up,
    w_down,
):
    asked = jnp.transpose(queries.reshape(8, 16, 4, HD), (1, 2, 0, 3)).reshape(16, 32, HD)
    pairs = jnp.stack([keys.reshape(8, KV, HD), values.reshape(8, KV, HD)], 0)
    pairs = jnp.transpose(pairs, (2, 0, 1, 3)).reshape(KV, 16, HD)
    message = jnp.concatenate([asked, jnp.repeat(pairs, 2, axis=0)], 1)
    gain = jnp.broadcast_to(norm_gain.astype(F32)[None, :], (8, 512))
    return run_block(
        offset, message, residual, gain, cache_keys, cache_values, w_out, w_gate, w_up, w_down
    )


def solution(mesh):
    in_specs = (
        P("sp", "tp"),
        P(("tp", "sp"), None),
        P(("tp", "sp"), None),
        P(("tp", "sp"), None),
        P("tp", None),
        P("tp", None),
        P(),
        P("sp", "tp"),
        P("tp"),
        P("tp", "sp"),
        P("tp", "sp"),
        P("sp", "tp"),
    )
    out_specs = P("sp", "tp")
    return jax.shard_map(
        per_device, mesh=mesh, in_specs=in_specs, out_specs=out_specs, check_vma=False
    )
```

time: 527 us -> 215 us (0.41)
  the two profiles are of different devices: /device:TPU:2 before, /device:TPU:1 now
where the time goes in v3:
time: 215 us
  Pallas kernels  209 us (97%)
  local copies, waits for them, and re-layouts  2.87 us (1%)
  other arithmetic  2.33 us (1%)
    pallas_call x1, Pallas kernels, run_block(): pl.pallas_call(block_kernel, out_shape=jax.ShapeDtypeStruct((128, 512), B...  209 us

profile of v3, /device:TPU:1, one launch (start us, length us, event | category | flops | bytes accessed | tf_op | source)
XLA Modules:
  0.0 215.1 jit_solution(15048065744784698851)
XLA Ops:
  0.7 1.3 broadcast_in_dim.10.gain_ref
  1.9 0.7 maximum_bitcast_fusion
  2.7 1.6 pad_maximum_fusion.message_ref
  4.3 209.2 %block.1 = bf16[128,512]{1,0:T(8,128)(2,1)} custom-call(s32[1]{0:T(128)S(6)} %copy.14.offset_ref, bf16[16,48,128]{2,1,0:T(8,128)(2,1)} %pad_maximum_fusion.message_ref, bf16[128,512]{1,0:T(8,128)(2,1)} %residual_ref.1, f32[8,512]{1,0:T(8,128)} %broadcast_in_dim.10.gain_ref, bf16[1024,1024]{1,0:T(8,128)(2,1)} %cache_k_ref.1, bf16[1024,1024]{1,0:T(8,128)(2,1)} %cache_v_ref.1, ...), custom_call_target="tpu_custom_call" | custom-call | tf_op jit(solution)/shard_map/block/pallas_call | solution.py:523
  213.5 1.6 copy.15
  (1 shorter events, 0.0 us)

commit v4 on v3

--- a/solution.py
+++ b/solution.py
@@ -35,13 +35,6 @@
 
 def tp_of(place, x):
     return ((place // 2) * 4 + x) * 2 + place % 2
-
-
-def greet(devices):
-    barrier = pltpu.get_barrier_semaphore()
-    for device in devices:
-        pl.semaphore_signal(barrier, inc=1, device_id=device, device_id_type=MESH)
-    pl.semaphore_wait(barrier, len(devices))
 
 
 class Spread:
@@ -71,10 +64,13 @@
         self.over.wait_recv()
         self.passed.start()
 
-    def finish(self):
+    def near(self):
         if self.local is not None:
             self.local.wait()
-        self.pair.wait()
+        self.pair.wait_recv()
+
+    def finish(self):
+        self.pair.wait_send()
         self.over.wait_send()
         self.passed.wait()
 
@@ -89,8 +85,12 @@
     for copy in copies:
         copy.start()
     blocks[x] = own[...]
-    for copy in copies:
-        copy.wait()
+
+    def settle():
+        for copy in copies:
+            copy.wait()
+
+    return settle
 
 
 def scatter_z(product, sent, got, cross_send, cross_recv, send_sem, recv_sem, cross_sem):
@@ -142,7 +142,7 @@
     return mine + cross_recv[...].astype(F32)
 
 
-def gather_z(own, blocks, send_sem, recv_sem, cross_sem):
+def gather_z(own, blocks, send_sem, recv_sem, cross_sem, beside):
     sp, tp = lax.axis_index("sp"), lax.axis_index("tp")
     z, low = sp // 2, sp % 2
     neighbours = (((sp + 2) % 16, tp), ((sp + 14) % 16, tp))
@@ -168,6 +168,7 @@
                 hop(way, distance, place, r).wait_recv()
                 if distance < 3 or r == way:
                     hop(way, distance + 1, place, r).start()
+        beside[distance]()
     for way in range(2):
         hop(way, 4, (z + 4) % 8, way).wait_recv()
     cross.wait_send()
@@ -180,7 +181,9 @@
 
 def block_kernel(
     offset_ref,
-    message_ref,
+    queries_ref,
+    keys_ref,
+    values_ref,
     residual_ref,
     gain_ref,
     cache_k_ref,
@@ -190,6 +193,8 @@
     w_up_ref,
     w_down_ref,
     out_ref,
+    message,
+    own_gain,
     received,
     keys,
     own_vals,
@@ -198,6 +203,9 @@
     new_vals_t,
     own_queries,
     queries,
+    tops,
+    totals,
+    sums,
     out_send,
     out_recv,
     stat_send,
@@ -256,14 +264,10 @@
     sp, tp = lax.axis_index("sp"), lax.axis_index("tp")
     high, x, core = tp // 8, (tp // 2) % 4, tp % 2
     place = high * 2 + core
-    greet([((sp + j) % 16, tp) for j in range(1, 16)] + [(sp, (tp + j) % 16) for j in range(1, 16)])
-
-    def exchange(j, _):
-        target = (sp + j) % 16
-        remote(message_ref.at[target], received.at[sp], a2a_send.at[j], a2a_recv.at[j], (target, tp)).start()
-        return 0
-
-    lax.fori_loop(1, 16, exchange, 0)
+    barrier = pltpu.get_barrier_semaphore()
+    peers = [((sp + j) % 16, tp) for j in range(1, 16)] + [(sp, (tp + j) % 16) for j in range(1, 16)]
+    for device in peers:
+        pl.semaphore_signal(barrier, inc=1, device_id=device, device_id_type=MESH)
     columns = pl.ds(pl.multiple_of((sp // 2) * HD, HD), HD)
     spread_k = Spread(cache_k_ref.at[:, columns], keys, spread_sem, 0)
     spread_v = Spread(vals_t.at[place], vals_t, spread_sem, 7, local=False)
@@ -273,16 +277,32 @@
     spread_d = Spread(w_down_ref, w_down, spread_sem, 35)
     load_v = pltpu.make_async_copy(cache_v_ref.at[:, columns], own_vals, small_sem.at[0])
     load_v.start()
-    spread_k.keep()
-    spread_k.send()
-    received[sp] = message_ref[sp]
+    for spread in (spread_k, spread_o, spread_g, spread_u, spread_d):
+        spread.keep()
+    for target in range(16):
+        lanes = target // 2 * HD
+        rows = [
+            queries_ref[:, target * 512 + h * HD : target * 512 + h * HD + HD].astype(F32) for h in range(4)
+        ]
+        rows.append(keys_ref[:, lanes : lanes + HD].astype(F32))
+        rows.append(values_ref[:, lanes : lanes + HD].astype(F32))
+        message[target] = jnp.concatenate(rows, 0).astype(BF)
+    own_gain[...] = jnp.broadcast_to(gain_ref[...].astype(F32), (8, 512))
     load_v.wait()
     for piece in range(4):
         rows = own_vals[piece * 256 : piece * 256 + 256, :].astype(F32)
         vals_t[place, :, piece * 256 : piece * 256 + 256] = rows.T.astype(BF)
+    pl.semaphore_wait(barrier, len(peers))
+
+    def exchange(j, _):
+        target = (sp + j) % 16
+        remote(message.at[target], received.at[sp], a2a_send.at[j], a2a_recv.at[j], (target, tp)).start()
+        return 0
+
+    lax.fori_loop(1, 16, exchange, 0)
+    spread_k.send()
     spread_v.send()
-    for spread in (spread_o, spread_g, spread_u, spread_d):
-        spread.keep()
+    received[sp] = message[sp]
 
     def arrived(j, _):
         block = received.at[(sp + 16 - j) % 16]
@@ -304,6 +324,7 @@
         return 0
 
     lax.fori_loop(0, 16, ask, 0)
+    spread_o.send()
     fresh = received[:, 32:, :].astype(F32).reshape(16, 2, 8, HD)
     new_keys[place] = fresh[:, 0].reshape(HD, HD).astype(BF)
     new_vals_t[place] = fresh[:, 1].reshape(HD, HD).T.astype(BF)
@@ -323,51 +344,61 @@
         smalls.append(to_quad(i, 0, new_keys.at[place], new_keys.at[place]))
         smalls.append(to_quad(i, 1, new_vals_t.at[place], new_vals_t.at[place]))
         smalls.append(to_quad(i, 2, residual_ref.at[rows], residuals.at[place]))
-        smalls.append(to_quad(i, 3, gain_ref, gains.at[place]))
+        smalls.append(to_quad(i, 3, own_gain, gains.at[place]))
     for copy in smalls:
         copy.start()
     residuals[place] = residual_ref[pl.ds(pl.multiple_of(place * 32, 32), 32)]
-    gains[place] = gain_ref[...]
-    spread_k.forward()
-    spread_v.forward()
-    spread_k.finish()
-    spread_v.finish()
-    for copy in smalls:
-        copy.wait()
-    spread_o.send()
-    spread_g.send()
-
-    def attend(k, _):
+    gains[place] = own_gain[...]
+    spread_k.near()
+    spread_v.near()
+
+    def attend(k, turn):
         asker = (x + 4 - k) % 4
-        for source in range(4):
-            j = (tp - tp_of(source, asker) + 16) % 16
-
-            @pl.when(j > 0)
+        if turn == 0:
+
+            @pl.when(k == 2)
             def _():
-                block = queries.at[asker, source]
-                remote(block, block, q_send.at[j], q_recv.at[j], (sp, tp)).wait_recv()
+                spread_k.forward()
+
+            @pl.when(k == 3)
+            def _():
+                spread_v.forward()
+
+            for source in range(4):
+                j = (tp - tp_of(source, asker) + 16) % 16
+
+                @pl.when(j > 0)
+                def _():
+                    block = queries.at[asker, source]
+                    remote(block, block, q_send.at[j], q_recv.at[j], (sp, tp)).wait_recv()
 
         q = queries[asker].reshape(512, HD)
-        top = jnp.full((1, 512), LOWEST, F32)
-        total = jnp.zeros((1, 512), F32)
-        summed = jnp.zeros((HD, 512), F32)
-        lane = lax.broadcasted_iota(jnp.int32, (128, 512), 1)
-        token = ((lane // 256) * 4 + asker) * 256 + ((lane // 128) % 2) * 128
-        token = token + place * 32 + ((lane // 32) % 4) * 8 + lane % 8
-        ahead = lax.broadcasted_iota(jnp.int32, (128, 512), 0) - token
-        for chunk in range(9):
-            held, first = chunk // 2, (chunk % 2) * 512
-            if chunk < 8:
+        if turn == 0:
+            top = jnp.full((1, 512), LOWEST, F32)
+            total = jnp.zeros((1, 512), F32)
+            summed = jnp.zeros((HD, 512), F32)
+        else:
+            top = tops[k, 0:1, :]
+            total = totals[k, 0:1, :]
+            summed = sums[k]
+        for chunk in range(4 + turn):
+            if chunk < 4:
+                held = (high + turn) % 2 * 2 + chunk // 2
+                first = (chunk % 2) * 512
                 block = keys[held, first : first + 512, :]
                 block_t = vals_t[held, :, first : first + 512]
             else:
                 block = new_keys[...].reshape(512, HD)
                 block_t = jnp.concatenate([new_vals_t[i] for i in range(4)], 1)
             scores = lax.dot_general(block, q, (((1,), (1,)), ((), ())), preferred_element_type=F32)
-            if chunk < 8:
+            if chunk < 4:
                 position = lax.broadcasted_iota(jnp.int32, (512, 512), 0)
                 scores = jnp.where(position < offset_ref[0] - tp_of(held, x) * 1024 - first, scores, LOWEST)
             else:
+                lane = lax.broadcasted_iota(jnp.int32, (128, 512), 1)
+                token = ((lane // 256) * 4 + asker) * 256 + ((lane // 128) % 2) * 128
+                token = token + place * 32 + ((lane // 32) % 4) * 8 + lane % 8
+                ahead = lax.broadcasted_iota(jnp.int32, (128, 512), 0) - token
                 scores = jnp.concatenate(
                     [
                         jnp.where(ahead <= -tp_of(i, x) * 128, scores[i * 128 : i * 128 + 128], LOWEST)
@@ -381,6 +412,11 @@
             total = total * factor + jnp.sum(weights, axis=0, keepdims=True)
             summed = summed * factor + jnp.dot(block_t, weights.astype(BF), preferred_element_type=F32)
             top = higher
+        if turn == 0:
+            tops[k] = jnp.broadcast_to(top, (8, 512))
+            totals[k] = jnp.broadcast_to(total, (8, 512))
+            sums[k] = summed
+            return
         out_send[k] = summed.astype(BF)
         stat_send[k] = jnp.concatenate([jnp.broadcast_to(top, (4, 512)), jnp.broadcast_to(total, (4, 512))], 0)
 
@@ -390,9 +426,21 @@
             remote(out_send.at[k], out_recv.at[k], o_send.at[k], o_recv.at[k], target).start()
             remote(stat_send.at[k], stat_recv.at[k], st_send.at[k], st_recv.at[k], target).start()
 
+    def attend_near(k, _):
+        attend(k, 0)
         return 0
 
-    lax.fori_loop(0, 4, attend, 0)
+    def attend_far(k, _):
+        attend((k + 1) % 4, 1)
+        return 0
+
+    lax.fori_loop(0, 4, attend_near, 0)
+    spread_g.send()
+    spread_k.finish()
+    spread_v.finish()
+    for copy in smalls:
+        copy.wait()
+    lax.fori_loop(0, 4, attend_far, 0)
     spread_o.forward()
     spread_u.send()
 
@@ -419,7 +467,9 @@
     mixed = (summed / total).T.reshape(16, 4, 8, HD)
     for h in range(4):
         own_attended[:, :, h * HD : (h + 1) * HD] = mixed[:, h].reshape(2, 64, HD).astype(BF)
-    gather_x(own_attended, attended, aa_send, aa_recv)
+    gather_x(own_attended, attended, aa_send, aa_recv)()
+    spread_d.send()
+    spread_o.near()
     spread_o.finish()
 
     def project(z):
@@ -432,8 +482,6 @@
         project, sent_a, got_a, cross_a.at[0], cross_a.at[1], za_send, za_recv, cross_sem.at[pl.ds(0, 2)]
     )
     spread_g.forward()
-    spread_u.forward()
-    spread_d.send()
     own_residual = jnp.concatenate([residuals[i] for i in range(4)], 1)
     stream[...] = (own_residual.astype(F32) + attn_out).astype(BF)
     wide = stream[...].astype(F32)
@@ -450,51 +498,79 @@
     scale = jnp.concatenate([lax.rsqrt(mean + EPS)] * 16, 1)
     gain = jnp.concatenate([gains[i, 0:1, :] for i in range(4)], 1)
     own_normed[...] = (stream[...].astype(F32) * scale * gain).astype(BF)
-    gather_z(own_normed, normed, zn_send, zn_recv, cross_sem.at[pl.ds(2, 2)])
-    spread_d.forward()
-    spread_g.finish()
-    spread_u.finish()
-
-    def part(column, up):
-        rows = normed[pl.ds(2 * ((x + column) % 4), 2)].reshape(128, 2048)
+    spread_u.forward()
+    for spread in (spread_g, spread_u):
+        spread.near()
+        spread.finish()
+    z = sp // 2
+
+    def part(turn, column, up):
+        rows = normed[(z + 7 + (x + column) % 4 + 4 * turn) % 8].reshape(64, 2048)
         weight = w_up if up else w_gate
         return jnp.dot(rows, weight[...].reshape(2048, 1024), preferred_element_type=F32)
 
     neighbours = ((sp, tp_of(place, (x + 1) % 4)), (sp, tp_of(place, (x + 3) % 4)))
 
-    def hop(which):
+    def hop(turn, which):
+        index = turn * 6 + which
         return remote(
-            x_sent.at[which], x_got.at[which], x_send.at[which], x_recv.at[which], neighbours[which // 3]
+            x_sent.at[index], x_got.at[index], x_send.at[index], x_recv.at[index], neighbours[which // 3]
         )
 
-    def post(which, value):
-        x_sent[which] = value.astype(BF)
-        hop(which).start()
-
-    def came(which):
-        hop(which).wait_recv()
-        return x_got[which].astype(F32)
-
-    post(0, part(2, False))
-    post(3, part(2, True))
-    post(2, part(1, True))
-    post(5, part(3, False))
-    second = part(1, False)
-    post(1, second + came(0))
-    second = part(3, True)
-    post(4, second + came(3))
-    gate = part(0, False)
-    up = part(0, True)
-    gate = gate + came(5) + came(1)
-    up = up + came(2) + came(4)
-    own_hidden[...] = (gate / (1.0 + jnp.exp(-gate)) * up).astype(BF).reshape(2, 64, 1024)
-    gather_x(own_hidden, hidden, ah_send, ah_recv)
+    def post(turn, which, value):
+        x_sent[turn * 6 + which] = value.astype(BF)
+        hop(turn, which).start()
+
+    def came(turn, which):
+        hop(turn, which).wait_recv()
+        return x_got[turn * 6 + which].astype(F32)
+
+    def open_turn(turn):
+        post(turn, 0, part(turn, 2, False))
+        post(turn, 3, part(turn, 2, True))
+        post(turn, 2, part(turn, 1, True))
+        post(turn, 5, part(turn, 3, False))
+
+    def pass_turn(turn):
+        second = part(turn, 1, False)
+        post(turn, 1, second + came(turn, 0))
+        second = part(turn, 3, True)
+        post(turn, 4, second + came(turn, 3))
+
+    def close_turn(turn):
+        gate = part(turn, 0, False)
+        up = part(turn, 0, True)
+        gate = gate + came(turn, 5) + came(turn, 1)
+        up = up + came(turn, 2) + came(turn, 4)
+        own_hidden[turn] = (gate / (1.0 + jnp.exp(-gate)) * up).astype(BF)
+        return gather_x(
+            own_hidden.at[turn], hidden.at[turn], ah_send.at[pl.ds(4 * turn, 4)], ah_recv.at[pl.ds(4 * turn, 4)]
+        )
+
+    gather_z(
+        own_normed,
+        normed,
+        zn_send,
+        zn_recv,
+        cross_sem.at[pl.ds(2, 2)],
+        {1: lambda: None, 2: lambda: open_turn(0), 3: lambda: pass_turn(0)},
+    )
+    open_turn(1)
+    first_half = close_turn(0)
+    pass_turn(1)
+    spread_d.forward()
+    second_half = close_turn(1)
+    first_half()
+    second_half()
+    spread_d.near()
     spread_d.finish()
-    for which in range(6):
-        hop(which).wait_send()
-
-    def down(z):
-        rows = hidden[z // 2, z % 2]
+    for turn in range(2):
+        for which in range(6):
+            hop(turn, which).wait_send()
+
+    def down(target):
+        offset = (target + 9 - z) % 8
+        rows = hidden[offset // 4, offset % 4]
         return jnp.concatenate(
             [jnp.dot(rows, w_down[i], preferred_element_type=F32) for i in range(4)], 1
         )
@@ -517,15 +593,17 @@
         copy.wait()
 
 
-def run_block(offset, message, residual, gain, cache_keys, cache_values, w_out, w_gate, w_up, w_down):
+def run_block(offset, queries, keys, values, residual, gain, cache_keys, cache_values, w_out, w_gate, w_up, w_down):
     hop = VM((2, 4, 2, 32, 2048), BF)
     vmem = pl.BlockSpec(memory_space=pltpu.VMEM)
     return pl.pallas_call(
         block_kernel,
         out_shape=jax.ShapeDtypeStruct((128, 512), BF),
-        in_specs=[pl.BlockSpec(memory_space=pltpu.SMEM)] + [vmem] * 3 + [pl.BlockSpec(memory_space=pl.ANY)] * 6,
+        in_specs=[pl.BlockSpec(memory_space=pltpu.SMEM)] + [vmem] * 5 + [pl.BlockSpec(memory_space=pl.ANY)] * 6,
         out_specs=vmem,
         scratch_shapes=[
+            VM((16, 48, HD), BF),
+            VM((8, 512), F32),
             VM((16, 48, HD), BF),
             VM((4, 1024, HD), BF),
             VM((1024, HD), BF),
@@ -534,6 +612,9 @@
             VM((4, HD, 128), BF),
             VM((4, 128, HD), BF),
             VM((4, 4, 128, HD), BF),
+            VM((4, 8, 512), F32),
+            VM((4, 8, 512), F32),
+            VM((4, HD, 512), F32),
             VM((4, HD, 512), BF),
             VM((4, HD, 512), BF),
             VM((4, 8, 512), F32),
@@ -557,10 +638,10 @@
             VM((4, 32, 128), F32),
             VM((32, 2048), BF),
             VM((8, 2, 32, 2048), BF),
-            VM((6, 128, 1024), BF),
-            VM((6, 128, 1024), BF),
+            VM((12, 64, 1024), BF),
+            VM((12, 64, 1024), BF),
             VM((2, 64, 1024), BF),
-            VM((4, 2, 64, 1024), BF),
+            VM((2, 4, 64, 1024), BF),
             VM((4, 32, 512), BF),
         ]
         + [DMA((16,))] * 2
@@ -570,15 +651,15 @@
         + [DMA((16,))] * 2
         + [DMA((4,))] * 2
         + [DMA((20,))] * 2
-        + [DMA((6,))] * 2
-        + [DMA((4,))] * 2
+        + [DMA((12,))] * 2
+        + [DMA((8,))] * 2
         + [DMA((16,))] * 2
         + [DMA((6,)), DMA((8,))],
         compiler_params=pltpu.CompilerParams(
             collective_id=0, has_side_effects=True, vmem_limit_bytes=VMEM_LIMIT
         ),
         name="block",
-    )(offset, message, residual, gain, cache_keys, cache_values, w_out, w_gate, w_up, w_down)
+    )(offset, queries, keys, values, residual, gain, cache_keys, cache_values, w_out, w_gate, w_up, w_down)
 
 
 def per_device(
@@ -595,13 +676,19 @@
     w_up,
     w_down,
 ):
-    asked = jnp.transpose(queries.reshape(8, 16, 4, HD), (1, 2, 0, 3)).reshape(16, 32, HD)
-    pairs = jnp.stack([keys.reshape(8, KV, HD), values.reshape(8, KV, HD)], 0)
-    pairs = jnp.transpose(pairs, (2, 0, 1, 3)).reshape(KV, 16, HD)
-    message = jnp.concatenate([asked, jnp.repeat(pairs, 2, axis=0)], 1)
-    gain = jnp.broadcast_to(norm_gain.astype(F32)[None, :], (8, 512))
     return run_block(
-        offset, message, residual, gain, cache_keys, cache_values, w_out, w_gate, w_up, w_down
+        offset,
+        queries,
+        keys,
+        values,
+        residual,
+        norm_gain.reshape(1, 512),
+        cache_keys,
+        cache_values,
+        w_out,
+        w_gate,
+        w_up,
+        w_down,
     )
 
 

time: 215 us -> 211 us (0.981)
  other arithmetic: 2.33 us -> 0 us
where the time goes in v4:
time: 211 us
  Pallas kernels  208 us (99%)
  local copies, waits for them, and re-layouts  2.83 us (1%)
    pallas_call x1, Pallas kernels, run_block(): pl.pallas_call(block_kernel, out_shape=jax.ShapeDtypeStruct((128, 512), B...  208 us

profile of v4, /device:TPU:1, one launch (start us, length us, event | category | flops | bytes accessed | tf_op | source)
XLA Modules:
  0.0 211.1 jit_solution(8196648938483050829)
XLA Ops:
  0.7 1.3 reshape.3.gain_ref
  1.9 207.6 %block.1 = bf16[128,512]{1,0:T(8,128)(2,1)} custom-call(s32[1]{0:T(128)S(6)} %copy.14.offset_ref, bf16[8,8192]{1,0:T(8,128)(2,1)} %queries_ref.1, bf16[8,1024]{1,0:T(8,128)(2,1)} %keys_ref.1, bf16[8,1024]{1,0:T(8,128)(2,1)} %values_ref.1, bf16[128,512]{1,0:T(8,128)(2,1)} %residual_ref.1, bf16[1,512]{1,0:T(2,128)(2,1)} %reshape.3.gain_ref, ...), custom_call_target="tpu_custom_call" | custom-call | tf_op jit(solution)/shard_map/block/pallas_call | solution.py:599
  209.6 1.6 copy.15

commit v5 on v4

--- a/solution.py
+++ b/solution.py
@@ -38,19 +38,17 @@
 
 
 class Spread:
-    def __init__(self, source, buffer, sems, first, local=True):
+    def __init__(self, source, buffer, sems, first, local=True, rows=None):
         sp, tp = lax.axis_index("sp"), lax.axis_index("tp")
         high, x, core = tp // 8, (tp // 2) % 4, tp % 2
-        self.sems = sems
-        self.first = first
-        self.buffer = buffer
         self.sibling = (sp, tp + 1 - 2 * core)
         opposite = (sp, (tp + 8) % 16)
-        mine = buffer.at[high * 2 + core]
+        at = (lambda i: buffer.at[i]) if rows is None else (lambda i: buffer.at[i, rows])
+        mine = at(high * 2 + core)
         self.local = pltpu.make_async_copy(source, mine, sems.at[first]) if local else None
         self.pair = remote(source, mine, sems.at[first + 1], sems.at[first + 2], self.sibling)
         self.over = remote(source, mine, sems.at[first + 3], sems.at[first + 4], opposite)
-        across = buffer.at[(1 - high) * 2 + core]
+        across = at((1 - high) * 2 + core)
         self.passed = remote(across, across, sems.at[first + 5], sems.at[first + 6], self.sibling)
 
     def keep(self):
@@ -93,7 +91,7 @@
     return settle
 
 
-def scatter_z(product, sent, got, cross_send, cross_recv, send_sem, recv_sem, cross_sem):
+def scatter_z(product, sent, got, cross_send, cross_recv, send_sem, recv_sem, cross_sem, beside=None):
     sp, tp = lax.axis_index("sp"), lax.axis_index("tp")
     z, low = sp // 2, sp % 2
     neighbours = (((sp + 2) % 16, tp), ((sp + 14) % 16, tp))
@@ -130,6 +128,8 @@
     cross_send[...] = away.astype(BF)
     cross = remote(cross_send, cross_recv, cross_sem.at[0], cross_sem.at[1], other)
     cross.start()
+    if beside is not None:
+        beside()
     for way in range(2):
         hop(way, 3, 1).wait_recv()
         mine = mine + got[way, 3, 1].astype(F32)
@@ -158,6 +158,7 @@
     cross.start()
     for way in range(2):
         hop(way, 1, z, 0).start()
+    beside[0]()
     remote(own, blocks.at[z, 1 - low], cross_sem.at[0], cross_sem.at[1], other).wait_recv()
     for way in range(2):
         hop(way, 1, z, 1).start()
@@ -273,11 +274,14 @@
     spread_v = Spread(vals_t.at[place], vals_t, spread_sem, 7, local=False)
     spread_o = Spread(w_out_ref, w_out, spread_sem, 14)
     spread_g = Spread(w_gate_ref, w_gate, spread_sem, 21)
-    spread_u = Spread(w_up_ref, w_up, spread_sem, 28)
-    spread_d = Spread(w_down_ref, w_down, spread_sem, 35)
+    spread_u = [
+        Spread(w_up_ref.at[first : first + count], w_up, spread_sem, index, rows=pl.ds(first, count))
+        for first, count, index in ((0, 256, 28), (256, 128, 35), (384, 128, 42))
+    ]
+    spread_d = Spread(w_down_ref, w_down, spread_sem, 49)
     load_v = pltpu.make_async_copy(cache_v_ref.at[:, columns], own_vals, small_sem.at[0])
     load_v.start()
-    for spread in (spread_k, spread_o, spread_g, spread_u, spread_d):
+    for spread in (spread_k, spread_o, spread_g, *spread_u, spread_d):
         spread.keep()
     for target in range(16):
         lanes = target // 2 * HD
@@ -287,7 +291,7 @@
         rows.append(keys_ref[:, lanes : lanes + HD].astype(F32))
         rows.append(values_ref[:, lanes : lanes + HD].astype(F32))
         message[target] = jnp.concatenate(rows, 0).astype(BF)
-    own_gain[...] = jnp.broadcast_to(gain_ref[...].astype(F32), (8, 512))
+    own_gain[...] = jnp.broadcast_to(gain_ref[...].astype(F32).reshape(1, 512), (8, 512))
     load_v.wait()
     for piece in range(4):
         rows = own_vals[piece * 256 : piece * 256 + 256, :].astype(F32)
@@ -301,7 +305,7 @@
 
     lax.fori_loop(1, 16, exchange, 0)
     spread_k.send()
-    spread_v.send()
+    spread_v.pair.start()
     received[sp] = message[sp]
 
     def arrived(j, _):
@@ -324,7 +328,7 @@
         return 0
 
     lax.fori_loop(0, 16, ask, 0)
-    spread_o.send()
+    spread_v.over.start()
     fresh = received[:, 32:, :].astype(F32).reshape(16, 2, 8, HD)
     new_keys[place] = fresh[:, 0].reshape(HD, HD).astype(BF)
     new_vals_t[place] = fresh[:, 1].reshape(HD, HD).T.astype(BF)
@@ -349,6 +353,7 @@
         copy.start()
     residuals[place] = residual_ref[pl.ds(pl.multiple_of(place * 32, 32), 32)]
     gains[place] = own_gain[...]
+    spread_o.send()
     spread_k.near()
     spread_v.near()
 
@@ -359,10 +364,6 @@
             @pl.when(k == 2)
             def _():
                 spread_k.forward()
-
-            @pl.when(k == 3)
-            def _():
-                spread_v.forward()
 
             for source in range(4):
                 j = (tp - tp_of(source, asker) + 16) % 16
@@ -435,6 +436,7 @@
         return 0
 
     lax.fori_loop(0, 4, attend_near, 0)
+    spread_v.forward()
     spread_g.send()
     spread_k.finish()
     spread_v.finish()
@@ -442,7 +444,7 @@
         copy.wait()
     lax.fori_loop(0, 4, attend_far, 0)
     spread_o.forward()
-    spread_u.send()
+    spread_u[0].send()
 
     def asked(j, _):
         remote(own_queries.at[0], queries.at[x, place], q_send.at[j], q_recv.at[j], (sp, tp)).wait_send()
@@ -468,7 +470,6 @@
     for h in range(4):
         own_attended[:, :, h * HD : (h + 1) * HD] = mixed[:, h].reshape(2, 64, HD).astype(BF)
     gather_x(own_attended, attended, aa_send, aa_recv)()
-    spread_d.send()
     spread_o.near()
     spread_o.finish()
 
@@ -479,9 +480,18 @@
         )
 
     attn_out = scatter_z(
-        project, sent_a, got_a, cross_a.at[0], cross_a.at[1], za_send, za_recv, cross_sem.at[pl.ds(0, 2)]
+        project,
+        sent_a,
+        got_a,
+        cross_a.at[0],
+        cross_a.at[1],
+        za_send,
+        za_recv,
+        cross_sem.at[pl.ds(0, 2)],
+        spread_u[1].send,
     )
     spread_g.forward()
+    spread_u[0].forward()
     own_residual = jnp.concatenate([residuals[i] for i in range(4)], 1)
     stream[...] = (own_residual.astype(F32) + attn_out).astype(BF)
     wide = stream[...].astype(F32)
@@ -498,11 +508,18 @@
     scale = jnp.concatenate([lax.rsqrt(mean + EPS)] * 16, 1)
     gain = jnp.concatenate([gains[i, 0:1, :] for i in range(4)], 1)
     own_normed[...] = (stream[...].astype(F32) * scale * gain).astype(BF)
-    spread_u.forward()
-    for spread in (spread_g, spread_u):
-        spread.near()
-        spread.finish()
     z = sp // 2
+
+    def send_rest():
+        spread_u[2].send()
+        spread_d.send()
+
+    def have_weights():
+        spread_u[2].forward()
+        for spread in (spread_g, *spread_u):
+            spread.near()
+            spread.finish()
+        open_turn(0)
 
     def part(turn, column, up):
         rows = normed[(z + 7 + (x + column) % 4 + 4 * turn) % 8].reshape(64, 2048)
@@ -553,13 +570,13 @@
         zn_send,
         zn_recv,
         cross_sem.at[pl.ds(2, 2)],
-        {1: lambda: None, 2: lambda: open_turn(0), 3: lambda: pass_turn(0)},
+        {0: send_rest, 1: spread_u[1].forward, 2: have_weights, 3: lambda: pass_turn(0)},
     )
     open_turn(1)
     first_half = close_turn(0)
     pass_turn(1)
+    second_half = close_turn(1)
     spread_d.forward()
-    second_half = close_turn(1)
     first_half()
     second_half()
     spread_d.near()
@@ -645,7 +662,7 @@
             VM((4, 32, 512), BF),
         ]
         + [DMA((16,))] * 2
-        + [DMA((42,)), DMA((25,))]
+        + [DMA((56,)), DMA((25,))]
         + [DMA((16,))] * 2
         + [DMA((4,))] * 6
         + [DMA((16,))] * 2
@@ -682,7 +699,7 @@
         keys,
         values,
         residual,
-        norm_gain.reshape(1, 512),
+        norm_gain,
         cache_keys,
         cache_values,
         w_out,

time: 211 us -> 179 us (0.85)
  Pallas kernels: 208 us -> 177 us
    pallas_call x1, Pallas kernels: 208 us -> 177 us  [run_block(): pl.pallas_call(block_kernel, out_shape=jax.ShapeDtypeStruct((128, 512), B...]
where the time goes in v5:
time: 179 us
  Pallas kernels  177 us (99%)
    pallas_call x1, Pallas kernels, run_block(): pl.pallas_call(block_kernel, out_shape=jax.ShapeDtypeStruct((128, 512), B...  177 us

profile of v5, /device:TPU:1, one launch (start us, length us, event | category | flops | bytes accessed | tf_op | source)
XLA Modules:
  0.0 179.4 jit_solution(14249427551331635464)
XLA Ops:
  0.7 177.1 %block.1 = bf16[128,512]{1,0:T(8,128)(2,1)} custom-call(s32[1]{0:T(128)S(6)} %copy.14.offset_ref, bf16[8,8192]{1,0:T(8,128)(2,1)} %queries_ref.1, bf16[8,1024]{1,0:T(8,128)(2,1)} %keys_ref.1, bf16[8,1024]{1,0:T(8,128)(2,1)} %values_ref.1, bf16[128,512]{1,0:T(8,128)(2,1)} %residual_ref.1, bf16[512]{0:T(512)(128)(2,1)} %gain_ref.1, ...), custom_call_target="tpu_custom_call" | custom-call | tf_op jit(solution)/shard_map/block/pallas_call | solution.py:616
  177.8 1.6 copy.15

commit v6 on v5

--- a/solution.py
+++ b/solution.py
@@ -73,25 +73,34 @@
         self.passed.wait()
 
 
-def gather_x(own, blocks, send_sem, recv_sem):
-    sp, tp = lax.axis_index("sp"), lax.axis_index("tp")
-    x, place = (tp // 2) % 4, (tp // 8) * 2 + tp % 2
-    copies = [
-        remote(own, blocks.at[x], send_sem.at[k], recv_sem.at[k], (sp, tp_of(place, (x + k) % 4)))
-        for k in (1, 3, 2)
-    ]
-    for copy in copies:
-        copy.start()
-    blocks[x] = own[...]
-
-    def settle():
-        for copy in copies:
-            copy.wait()
-
-    return settle
-
-
-def scatter_z(product, sent, got, cross_send, cross_recv, send_sem, recv_sem, cross_sem, beside=None):
+class GatherX:
+    def __init__(self, own, blocks, send_sem, recv_sem):
+        sp, tp = lax.axis_index("sp"), lax.axis_index("tp")
+        x, place = (tp // 2) % 4, (tp // 8) * 2 + tp % 2
+        self.x = x
+        self.blocks = blocks
+        self.copies = {
+            k: remote(own, blocks.at[x], send_sem.at[k], recv_sem.at[k], (sp, tp_of(place, (x + k) % 4)))
+            for k in (1, 3, 2)
+        }
+        self.incoming = lambda k, block: remote(own, block, send_sem.at[k], recv_sem.at[k], (sp, tp))
+        for copy in self.copies.values():
+            copy.start()
+        blocks[x] = own[...]
+
+    def have(self, source):
+        k = (self.x + 4 - source) % 4
+
+        @pl.when(k > 0)
+        def _():
+            self.incoming(k, self.blocks.at[source]).wait_recv()
+
+    def sent(self):
+        for copy in self.copies.values():
+            copy.wait_send()
+
+
+def scatter_z(product, sent, got, cross_send, cross_recv, send_sem, recv_sem, cross_sem):
     sp, tp = lax.axis_index("sp"), lax.axis_index("tp")
     z, low = sp // 2, sp % 2
     neighbours = (((sp + 2) % 16, tp), ((sp + 14) % 16, tp))
@@ -128,8 +137,6 @@
     cross_send[...] = away.astype(BF)
     cross = remote(cross_send, cross_recv, cross_sem.at[0], cross_sem.at[1], other)
     cross.start()
-    if beside is not None:
-        beside()
     for way in range(2):
         hop(way, 3, 1).wait_recv()
         mine = mine + got[way, 3, 1].astype(F32)
@@ -196,6 +203,7 @@
     out_ref,
     message,
     own_gain,
+    hides,
     received,
     keys,
     own_vals,
@@ -228,7 +236,9 @@
     cross_d,
     own_squares,
     squares,
-    own_normed,
+    own_scale,
+    scales,
+    streams,
     normed,
     x_sent,
     x_got,
@@ -261,6 +271,8 @@
     zd_recv,
     cross_sem,
     back_sem,
+    sc_send,
+    sc_recv,
 ):
     sp, tp = lax.axis_index("sp"), lax.axis_index("tp")
     high, x, core = tp // 8, (tp // 2) % 4, tp % 2
@@ -292,6 +304,10 @@
         rows.append(values_ref[:, lanes : lanes + HD].astype(F32))
         message[target] = jnp.concatenate(rows, 0).astype(BF)
     own_gain[...] = jnp.broadcast_to(gain_ref[...].astype(F32).reshape(1, 512), (8, 512))
+    for i in range(4):
+        lane = lax.broadcasted_iota(jnp.int32, (1024, HD), 1)
+        position = lax.broadcasted_iota(jnp.int32, (1024, HD), 0) + tp_of(i, x) * 1024
+        hides[i] = jnp.where((lane == 0) & (position >= offset_ref[0]), LOWEST, 0.0).astype(BF)
     load_v.wait()
     for piece in range(4):
         rows = own_vals[piece * 256 : piece * 256 + 256, :].astype(F32)
@@ -374,6 +390,7 @@
                     remote(block, block, q_send.at[j], q_recv.at[j], (sp, tp)).wait_recv()
 
         q = queries[asker].reshape(512, HD)
+        marked = jnp.concatenate([q, jnp.ones((512, HD), BF)], 1)
         if turn == 0:
             top = jnp.full((1, 512), LOWEST, F32)
             total = jnp.zeros((1, 512), F32)
@@ -386,16 +403,17 @@
             if chunk < 4:
                 held = (high + turn) % 2 * 2 + chunk // 2
                 first = (chunk % 2) * 512
-                block = keys[held, first : first + 512, :]
+                block = jnp.concatenate(
+                    [keys[held, first : first + 512, :], hides[held, first : first + 512, :]], 1
+                )
                 block_t = vals_t[held, :, first : first + 512]
             else:
                 block = new_keys[...].reshape(512, HD)
                 block_t = jnp.concatenate([new_vals_t[i] for i in range(4)], 1)
-            scores = lax.dot_general(block, q, (((1,), (1,)), ((), ())), preferred_element_type=F32)
-            if chunk < 4:
-                position = lax.broadcasted_iota(jnp.int32, (512, 512), 0)
-                scores = jnp.where(position < offset_ref[0] - tp_of(held, x) * 1024 - first, scores, LOWEST)
-            else:
+            scores = lax.dot_general(
+                block, marked if chunk < 4 else q, (((1,), (1,)), ((), ())), preferred_element_type=F32
+            )
+            if chunk == 4:
                 lane = lax.broadcasted_iota(jnp.int32, (128, 512), 1)
                 token = ((lane // 256) * 4 + asker) * 256 + ((lane // 128) % 2) * 128
                 token = token + place * 32 + ((lane // 32) % 4) * 8 + lane % 8
@@ -469,12 +487,17 @@
     mixed = (summed / total).T.reshape(16, 4, 8, HD)
     for h in range(4):
         own_attended[:, :, h * HD : (h + 1) * HD] = mixed[:, h].reshape(2, 64, HD).astype(BF)
-    gather_x(own_attended, attended, aa_send, aa_recv)()
+    whole = GatherX(own_attended, attended, aa_send, aa_recv)
     spread_o.near()
     spread_o.finish()
 
-    def project(z):
-        rows = attended[z % 4, z // 4]
+    awaited = [0, 0]
+
+    def project(target):
+        if awaited[0] < 4:
+            whole.have(target % 4)
+            awaited[0] += 1
+        rows = attended[target % 4, target // 4]
         return jnp.concatenate(
             [jnp.dot(rows, w_out[i], preferred_element_type=F32) for i in range(4)], 1
         )
@@ -488,8 +511,8 @@
         za_send,
         za_recv,
         cross_sem.at[pl.ds(0, 2)],
-        spread_u[1].send,
     )
+    whole.sent()
     spread_g.forward()
     spread_u[0].forward()
     own_residual = jnp.concatenate([residuals[i] for i in range(4)], 1)
@@ -502,24 +525,58 @@
     ]
     for copy in tells:
         copy.start()
-    for copy in tells:
-        copy.wait()
-    mean = (own_squares[...] + squares[1] + squares[2] + squares[3]) / D
-    scale = jnp.concatenate([lax.rsqrt(mean + EPS)] * 16, 1)
-    gain = jnp.concatenate([gains[i, 0:1, :] for i in range(4)], 1)
-    own_normed[...] = (stream[...].astype(F32) * scale * gain).astype(BF)
     z = sp // 2
 
     def send_rest():
+        spread_u[1].send()
+        for copy in tells:
+            copy.wait()
+        mean = (own_squares[...] + squares[1] + squares[2] + squares[3]) / D
+        own_scale[...] = jnp.concatenate([lax.rsqrt(mean + EPS)] * 4, 0).T[:8]
+        scales[sp] = own_scale[...]
+
+        def tell_scale(j, _):
+            device = ((sp + j) % 16, tp)
+            remote(own_scale, scales.at[sp], sc_send.at[j], sc_recv.at[j], device).start()
+            return 0
+
+        lax.fori_loop(1, 16, tell_scale, 0)
         spread_u[2].send()
         spread_d.send()
 
-    def have_weights():
+    def normalise(turn):
+        gain = jnp.concatenate([gains[i, 0:1, :] for i in range(4)], 1)
+
+        def one(i, _):
+            source = (z + 7 + i // 2 + 4 * turn) % 8
+            scale = jnp.broadcast_to(scales[source * 2 + i % 2, 0:1, :], (128, 128)).T[:32]
+            scale = jnp.concatenate([scale] * 16, 1)
+            normed[source, i % 2] = (streams[source, i % 2].astype(F32) * scale * gain).astype(BF)
+            return 0
+
+        lax.fori_loop(0, 8, one, 0)
+
+    def start_gate():
+        spread_u[1].forward()
+        spread_g.near()
+        spread_g.finish()
+
+        def told_scale(j, _):
+            block = scales.at[(sp + 16 - j) % 16]
+            remote(own_scale, block, sc_send.at[j], sc_recv.at[j], (sp, tp)).wait()
+            return 0
+
+        lax.fori_loop(1, 16, told_scale, 0)
+        normalise(0)
+        open_gate(0)
+
+    def start_up():
+        pass_gate(0)
         spread_u[2].forward()
-        for spread in (spread_g, *spread_u):
+        for spread in spread_u:
             spread.near()
             spread.finish()
-        open_turn(0)
+        open_up(0)
 
     def part(turn, column, up):
         rows = normed[(z + 7 + (x + column) % 4 + 4 * turn) % 8].reshape(64, 2048)
@@ -542,15 +599,19 @@
         hop(turn, which).wait_recv()
         return x_got[turn * 6 + which].astype(F32)
 
-    def open_turn(turn):
+    def open_gate(turn):
         post(turn, 0, part(turn, 2, False))
+        post(turn, 5, part(turn, 3, False))
+
+    def open_up(turn):
         post(turn, 3, part(turn, 2, True))
         post(turn, 2, part(turn, 1, True))
-        post(turn, 5, part(turn, 3, False))
-
-    def pass_turn(turn):
+
+    def pass_gate(turn):
         second = part(turn, 1, False)
         post(turn, 1, second + came(turn, 0))
+
+    def pass_up(turn):
         second = part(turn, 3, True)
         post(turn, 4, second + came(turn, 3))
 
@@ -560,25 +621,27 @@
         gate = gate + came(turn, 5) + came(turn, 1)
         up = up + came(turn, 2) + came(turn, 4)
         own_hidden[turn] = (gate / (1.0 + jnp.exp(-gate)) * up).astype(BF)
-        return gather_x(
+        return GatherX(
             own_hidden.at[turn], hidden.at[turn], ah_send.at[pl.ds(4 * turn, 4)], ah_recv.at[pl.ds(4 * turn, 4)]
         )
 
     gather_z(
-        own_normed,
-        normed,
+        stream,
+        streams,
         zn_send,
         zn_recv,
         cross_sem.at[pl.ds(2, 2)],
-        {0: send_rest, 1: spread_u[1].forward, 2: have_weights, 3: lambda: pass_turn(0)},
+        {0: send_rest, 1: lambda: None, 2: start_gate, 3: start_up},
     )
-    open_turn(1)
+    normalise(1)
+    open_gate(1)
+    open_up(1)
+    pass_up(0)
+    pass_gate(1)
     first_half = close_turn(0)
-    pass_turn(1)
+    pass_up(1)
     second_half = close_turn(1)
     spread_d.forward()
-    first_half()
-    second_half()
     spread_d.near()
     spread_d.finish()
     for turn in range(2):
@@ -586,7 +649,9 @@
             hop(turn, which).wait_send()
 
     def down(target):
-        offset = (target + 9 - z) % 8
+        offset = (5, 4, 6, 3, 7, 2, 0, 1)[awaited[1]]
+        awaited[1] += 1
+        (first_half, second_half)[offset // 4].have(offset % 4)
         rows = hidden[offset // 4, offset % 4]
         return jnp.concatenate(
             [jnp.dot(rows, w_down[i], preferred_element_type=F32) for i in range(4)], 1
@@ -595,6 +660,8 @@
     added = scatter_z(
         down, sent_d, got_d, cross_d.at[0], cross_d.at[1], zd_send, zd_recv, cross_sem.at[pl.ds(4, 2)]
     )
+    first_half.sent()
+    second_half.sent()
     result = (stream[...].astype(F32) + added).astype(BF)
     for i in range(4):
         own_out[i] = result[:, i * 512 : i * 512 + 512]
@@ -621,6 +688,7 @@
         scratch_shapes=[
             VM((16, 48, HD), BF),
             VM((8, 512), F32),
+            VM((4, 1024, HD), BF),
             VM((16, 48, HD), BF),
             VM((4, 1024, HD), BF),
             VM((1024, HD), BF),
@@ -653,7 +721,9 @@
             VM((2, 32, 2048), BF),
             VM((32, 128), F32),
             VM((4, 32, 128), F32),
-            VM((32, 2048), BF),
+            VM((8, 128), F32),
+            VM((16, 8, 128), F32),
+            VM((8, 2, 32, 2048), BF),
             VM((8, 2, 32, 2048), BF),
             VM((12, 64, 1024), BF),
             VM((12, 64, 1024), BF),
@@ -671,7 +741,7 @@
         + [DMA((12,))] * 2
         + [DMA((8,))] * 2
         + [DMA((16,))] * 2
-        + [DMA((6,)), DMA((8,))],
+        + [DMA((6,)), DMA((8,)), DMA((16,)), DMA((16,))],
         compiler_params=pltpu.CompilerParams(
             collective_id=0, has_side_effects=True, vmem_limit_bytes=VMEM_LIMIT
         ),

time: 179 us -> 180 us (level)
  no operation moved by 1% of the time
where the time goes in v6:
time: 180 us; the launch traced here: 179 us
  Pallas kernels  177 us (98%)
    pallas_call x1, Pallas kernels, run_block(): pl.pallas_call(block_kernel, out_shape=jax.ShapeDtypeStruct((128, 512), B...  177 us

profile of v6, /device:TPU:1, one launch (start us, length us, event | category | flops | bytes accessed | tf_op | source)
XLA Modules:
  0.0 179.0 jit_solution(8753620760582364631)
XLA Ops:
  0.7 176.8 %block.1 = bf16[128,512]{1,0:T(8,128)(2,1)} custom-call(s32[1]{0:T(128)S(6)} %copy.14.offset_ref, bf16[8,8192]{1,0:T(8,128)(2,1)} %queries_ref.1, bf16[8,1024]{1,0:T(8,128)(2,1)} %keys_ref.1, bf16[8,1024]{1,0:T(8,128)(2,1)} %values_ref.1, bf16[128,512]{1,0:T(8,128)(2,1)} %residual_ref.1, bf16[512]{0:T(512)(128)(2,1)} %gain_ref.1, ...), custom_call_target="tpu_custom_call" | custom-call | tf_op jit(solution)/shard_map/block/pallas_call | solution.py:683
  177.5 1.6 copy.15

commit v7 on v6

--- a/solution.py
+++ b/solution.py
@@ -106,45 +106,57 @@
     neighbours = (((sp + 2) % 16, tp), ((sp + 14) % 16, tp))
     other = (sp + 1 - 2 * low, tp)
 
-    def hop(way, step, r):
-        index = way * 8 + step * 2 + r
+    def hop(way, step, r, h):
         return remote(
-            sent.at[way, step, r], got.at[way, step, r], send_sem.at[index], recv_sem.at[index], neighbours[way]
+            sent.at[way, step, r, h],
+            got.at[way, step, r, h],
+            send_sem.at[way * 16 + step * 4 + r * 2 + h],
+            recv_sem.at[way * 16 + step * 4 + r * 2 + h],
+            neighbours[way],
         )
+
+    def post(way, step, r, h, piece):
+        sent[way, step, r, h] = piece.astype(BF)
+        hop(way, step, r, h).start()
 
     def split(place):
         part = product(place)
         return jnp.where(low == 0, part[32:], part[:32]), jnp.where(low == 0, part[:32], part[32:])
 
     far = split((z + 4) % 8)
-    for way in range(2):
-        sent[way, 0, way] = far[way].astype(BF)
-        hop(way, 0, way).start()
+    for r in range(2):
+        for way in range(2):
+            post(way, 0, r, way, far[r][way * 16 : way * 16 + 16])
     for step in range(1, 4):
         parts = [split((z + 4 - step) % 8), split((z + 4 + step) % 8)]
         for r in range(2):
+            for late in range(2):
+                for way in range(2):
+                    h = way if late else 1 - way
+                    piece = parts[way][r][h * 16 : h * 16 + 16]
+                    if step > 1 or late:
+                        hop(way, step - 1, r, h).wait_recv()
+                        piece = piece + got[way, step - 1, r, h].astype(F32)
+                    post(way, step, r, h, piece)
+    away, mine = split(z)
+
+    def arrived(r):
+        for late in range(2):
             for way in range(2):
-                piece = parts[way][r]
-                if step > 1 or r == way:
-                    hop(way, step - 1, r).wait_recv()
-                    piece = piece + got[way, step - 1, r].astype(F32)
-                sent[way, step, r] = piece.astype(BF)
-                hop(way, step, r).start()
-    away, mine = split(z)
-    for way in range(2):
-        hop(way, 3, 0).wait_recv()
-        away = away + got[way, 3, 0].astype(F32)
+                hop(way, 3, r, way if late else 1 - way).wait_recv()
+        return got[0, 3, r].reshape(32, 2048).astype(F32) + got[1, 3, r].reshape(32, 2048).astype(F32)
+
+    away = away + arrived(0)
     cross_send[...] = away.astype(BF)
     cross = remote(cross_send, cross_recv, cross_sem.at[0], cross_sem.at[1], other)
     cross.start()
+    mine = mine + arrived(1)
     for way in range(2):
-        hop(way, 3, 1).wait_recv()
-        mine = mine + got[way, 3, 1].astype(F32)
-    for way in range(2):
-        hop(way, 0, way).wait_send()
-        for step in range(1, 4):
-            for r in range(2):
-                hop(way, step, r).wait_send()
+        for r in range(2):
+            hop(way, 0, r, way).wait_send()
+            for step in range(1, 4):
+                for h in range(2):
+                    hop(way, step, r, h).wait_send()
     cross.wait()
     return mine + cross_recv[...].astype(F32)
 
@@ -155,36 +167,48 @@
     neighbours = (((sp + 2) % 16, tp), ((sp + 14) % 16, tp))
     other = (sp + 1 - 2 * low, tp)
 
-    def hop(way, distance, place, r):
-        block = blocks.at[place, low if r == 0 else 1 - low]
-        index = way * 10 + distance * 2 + r
+    def hop(way, distance, place, r, h):
+        block = blocks.at[place, low if r == 0 else 1 - low, pl.ds(h * 16, 16)]
+        index = way * 20 + distance * 4 + r * 2 + h
         return remote(block, block, send_sem.at[index], recv_sem.at[index], neighbours[way])
 
+    def cross(source, h):
+        rows = pl.ds(h * 16, 16)
+        return remote(
+            own.at[rows], blocks.at[z, source, rows], cross_sem.at[2 * h], cross_sem.at[2 * h + 1], other
+        )
+
+    for h in range(2):
+        cross(low, h).start()
     blocks[z, low] = own[...]
-    cross = remote(own, blocks.at[z, low], cross_sem.at[0], cross_sem.at[1], other)
-    cross.start()
-    for way in range(2):
-        hop(way, 1, z, 0).start()
-    beside[0]()
-    remote(own, blocks.at[z, 1 - low], cross_sem.at[0], cross_sem.at[1], other).wait_recv()
-    for way in range(2):
-        hop(way, 1, z, 1).start()
+    for h in range(2):
+        for way in range(2):
+            hop(way, 1, z, 0, h).start()
+    for h in range(2):
+        cross(1 - low, h).wait_recv()
+        for way in range(2):
+            hop(way, 1, z, 1, h).start()
+        if h == 0:
+            beside[0]()
     for distance in range(1, 4):
         for r in range(2):
-            for way in range(2):
-                place = (z + (8 - distance if way == 0 else distance)) % 8
-                hop(way, distance, place, r).wait_recv()
-                if distance < 3 or r == way:
-                    hop(way, distance + 1, place, r).start()
+            for h in range(2):
+                for way in range(2):
+                    place = (z + (8 - distance if way == 0 else distance)) % 8
+                    hop(way, distance, place, r, h).wait_recv()
+                    if distance < 3 or r == way:
+                        hop(way, distance + 1, place, r, h).start()
         beside[distance]()
     for way in range(2):
-        hop(way, 4, (z + 4) % 8, way).wait_recv()
-    cross.wait_send()
-    for way in range(2):
-        for distance in range(1, 4):
-            for r in range(2):
-                hop(way, distance, z, r).wait_send()
-        hop(way, 4, z, way).wait_send()
+        for h in range(2):
+            hop(way, 4, (z + 4) % 8, way, h).wait_recv()
+    for h in range(2):
+        cross(low, h).wait_send()
+        for way in range(2):
+            for distance in range(1, 4):
+                for r in range(2):
+                    hop(way, distance, z, r, h).wait_send()
+            hop(way, 4, z, way, h).wait_send()
 
 
 def block_kernel(
@@ -461,7 +485,6 @@
     for copy in smalls:
         copy.wait()
     lax.fori_loop(0, 4, attend_far, 0)
-    spread_o.forward()
     spread_u[0].send()
 
     def asked(j, _):
@@ -488,6 +511,7 @@
     for h in range(4):
         own_attended[:, :, h * HD : (h + 1) * HD] = mixed[:, h].reshape(2, 64, HD).astype(BF)
     whole = GatherX(own_attended, attended, aa_send, aa_recv)
+    spread_o.forward()
     spread_o.near()
     spread_o.finish()
 
@@ -630,7 +654,7 @@
         streams,
         zn_send,
         zn_recv,
-        cross_sem.at[pl.ds(2, 2)],
+        cross_sem.at[pl.ds(4, 4)],
         {0: send_rest, 1: lambda: None, 2: start_gate, 3: start_up},
     )
     normalise(1)
@@ -658,7 +682,7 @@
         )
 
     added = scatter_z(
-        down, sent_d, got_d, cross_d.at[0], cross_d.at[1], zd_send, zd_recv, cross_sem.at[pl.ds(4, 2)]
+        down, sent_d, got_d, cross_d.at[0], cross_d.at[1], zd_send, zd_recv, cross_sem.at[pl.ds(2, 2)]
     )
     first_half.sent()
     second_half.sent()
@@ -678,7 +702,7 @@
 
 
 def run_block(offset, queries, keys, values, residual, gain, cache_keys, cache_values, w_out, w_gate, w_up, w_down):
-    hop = VM((2, 4, 2, 32, 2048), BF)
+    hop = VM((2, 4, 2, 2, 16, 2048), BF)
     vmem = pl.BlockSpec(memory_space=pltpu.VMEM)
     return pl.pallas_call(
         block_kernel,
@@ -735,13 +759,13 @@
         + [DMA((56,)), DMA((25,))]
         + [DMA((16,))] * 2
         + [DMA((4,))] * 6
-        + [DMA((16,))] * 2
+        + [DMA((32,))] * 2
         + [DMA((4,))] * 2
-        + [DMA((20,))] * 2
+        + [DMA((40,))] * 2
         + [DMA((12,))] * 2
         + [DMA((8,))] * 2
-        + [DMA((16,))] * 2
-        + [DMA((6,)), DMA((8,)), DMA((16,)), DMA((16,))],
+        + [DMA((32,))] * 2
+        + [DMA((8,)), DMA((8,)), DMA((16,)), DMA((16,))],
         compiler_params=pltpu.CompilerParams(
             collective_id=0, has_side_effects=True, vmem_limit_bytes=VMEM_LIMIT
         ),

time: 180 us -> 178 us (0.989)
  Pallas kernels: 177 us -> 175 us
where the time goes in v7:
time: 178 us
  Pallas kernels  175 us (98%)
    pallas_call x1, Pallas kernels, run_block(): pl.pallas_call(block_kernel, out_shape=jax.ShapeDtypeStruct((128, 512), B...  175 us

profile of v7, /device:TPU:1, one launch (start us, length us, event | category | flops | bytes accessed | tf_op | source)
XLA Modules:
  0.0 177.7 jit_solution(3595398568334595324)
XLA Ops:
  0.7 175.4 %block.1 = bf16[128,512]{1,0:T(8,128)(2,1)} custom-call(s32[1]{0:T(128)S(6)} %copy.14.offset_ref, bf16[8,8192]{1,0:T(8,128)(2,1)} %queries_ref.1, bf16[8,1024]{1,0:T(8,128)(2,1)} %keys_ref.1, bf16[8,1024]{1,0:T(8,128)(2,1)} %values_ref.1, bf16[128,512]{1,0:T(8,128)(2,1)} %residual_ref.1, bf16[512]{0:T(512)(128)(2,1)} %gain_ref.1, ...), custom_call_target="tpu_custom_call" | custom-call | tf_op jit(solution)/shard_map/block/pallas_call | solution.py:707
  176.1 1.6 copy.15

commit v8 on v7

--- a/solution.py
+++ b/solution.py
@@ -568,17 +568,15 @@
         spread_u[2].send()
         spread_d.send()
 
-    def normalise(turn):
+    def normalise(turn, members):
         gain = jnp.concatenate([gains[i, 0:1, :] for i in range(4)], 1)
 
-        def one(i, _):
-            source = (z + 7 + i // 2 + 4 * turn) % 8
-            scale = jnp.broadcast_to(scales[source * 2 + i % 2, 0:1, :], (128, 128)).T[:32]
-            scale = jnp.concatenate([scale] * 16, 1)
-            normed[source, i % 2] = (streams[source, i % 2].astype(F32) * scale * gain).astype(BF)
-            return 0
-
-        lax.fori_loop(0, 8, one, 0)
+        for member in members:
+            source = (z + 7 + member + 4 * turn) % 8
+            for b in range(2):
+                scale = jnp.broadcast_to(scales[source * 2 + b, 0:1, :], (128, 128)).T[:32]
+                scale = jnp.concatenate([scale] * 16, 1)
+                normed[source, b] = (streams[source, b].astype(F32) * scale * gain).astype(BF)
 
     def start_gate():
         spread_u[1].forward()
@@ -591,7 +589,7 @@
             return 0
 
         lax.fori_loop(1, 16, told_scale, 0)
-        normalise(0)
+        normalise(0, (0, 1, 2, 3))
         open_gate(0)
 
     def start_up():
@@ -601,6 +599,7 @@
             spread.near()
             spread.finish()
         open_up(0)
+        normalise(1, (3, 0, 2))
 
     def part(turn, column, up):
         rows = normed[(z + 7 + (x + column) % 4 + 4 * turn) % 8].reshape(64, 2048)
@@ -657,13 +656,13 @@
         cross_sem.at[pl.ds(4, 4)],
         {0: send_rest, 1: lambda: None, 2: start_gate, 3: start_up},
     )
-    normalise(1)
+    normalise(1, (1,))
     open_gate(1)
     open_up(1)
     pass_up(0)
     pass_gate(1)
+    pass_up(1)
     first_half = close_turn(0)
-    pass_up(1)
     second_half = close_turn(1)
     spread_d.forward()
     spread_d.near()

time: 178 us -> 176 us (0.989)
  Pallas kernels: 175 us -> 172 us
    pallas_call x1, Pallas kernels: 175 us -> 172 us  [run_block(): pl.pallas_call(block_kernel, out_shape=jax.ShapeDtypeStruct((128, 512), B...]
where the time goes in v8:
time: 176 us; the launch traced here: 175 us
  Pallas kernels  172 us (98%)
    pallas_call x1, Pallas kernels, run_block(): pl.pallas_call(block_kernel, out_shape=jax.ShapeDtypeStruct((128, 512), B...  172 us

profile of v8, /device:TPU:1, one launch (start us, length us, event | category | flops | bytes accessed | tf_op | source)
XLA Modules:
  0.0 174.6 jit_solution(11780822608616086756)
XLA Ops:
  0.7 172.4 %block.1 = bf16[128,512]{1,0:T(8,128)(2,1)} custom-call(s32[1]{0:T(128)S(6)} %copy.14.offset_ref, bf16[8,8192]{1,0:T(8,128)(2,1)} %queries_ref.1, bf16[8,1024]{1,0:T(8,128)(2,1)} %keys_ref.1, bf16[8,1024]{1,0:T(8,128)(2,1)} %values_ref.1, bf16[128,512]{1,0:T(8,128)(2,1)} %residual_ref.1, bf16[512]{0:T(512)(128)(2,1)} %gain_ref.1, ...), custom_call_target="tpu_custom_call" | custom-call | tf_op jit(solution)/shard_map/block/pallas_call | solution.py:706
  173.1 1.6 copy.15

commit v9 on v8

--- a/solution.py
+++ b/solution.py
@@ -578,7 +578,7 @@
                 scale = jnp.concatenate([scale] * 16, 1)
                 normed[source, b] = (streams[source, b].astype(F32) * scale * gain).astype(BF)
 
-    def start_gate():
+    def have_scales():
         spread_u[1].forward()
         spread_g.near()
         spread_g.finish()
@@ -589,7 +589,10 @@
             return 0
 
         lax.fori_loop(1, 16, told_scale, 0)
-        normalise(0, (0, 1, 2, 3))
+        normalise(0, (1, 0, 2))
+
+    def start_gate():
+        normalise(0, (3,))
         open_gate(0)
 
     def start_up():
@@ -654,7 +657,7 @@
         zn_send,
         zn_recv,
         cross_sem.at[pl.ds(4, 4)],
-        {0: send_rest, 1: lambda: None, 2: start_gate, 3: start_up},
+        {0: send_rest, 1: have_scales, 2: start_gate, 3: start_up},
     )
     normalise(1, (1,))
     open_gate(1)

time: 176 us -> 175 us (level)
  no operation moved by 1% of the time
where the time goes in v9:
time: 175 us; the launch traced here: 174 us
  Pallas kernels  172 us (98%)
    pallas_call x1, Pallas kernels, run_block(): pl.pallas_call(block_kernel, out_shape=jax.ShapeDtypeStruct((128, 512), B...  172 us

profile of v9, /device:TPU:1, one launch (start us, length us, event | category | flops | bytes accessed | tf_op | source)
XLA Modules:
  0.0 174.1 jit_solution(13294877053934137304)
XLA Ops:
  0.7 171.9 %block.1 = bf16[128,512]{1,0:T(8,128)(2,1)} custom-call(s32[1]{0:T(128)S(6)} %copy.14.offset_ref, bf16[8,8192]{1,0:T(8,128)(2,1)} %queries_ref.1, bf16[8,1024]{1,0:T(8,128)(2,1)} %keys_ref.1, bf16[8,1024]{1,0:T(8,128)(2,1)} %values_ref.1, bf16[128,512]{1,0:T(8,128)(2,1)} %residual_ref.1, bf16[512]{0:T(512)(128)(2,1)} %gain_ref.1, ...), custom_call_target="tpu_custom_call" | custom-call | tf_op jit(solution)/shard_map/block/pallas_call | solution.py:709
  172.6 1.6 copy.15
